TPU v7x, 32 devices: a whole 2x2x4 slice. The times are simulated.
32 devices in a mesh: ctx: 8 (over z, x), shard: 4 (over y, core).
Axes of the slice: x: 2, y: 2, z: 4, core: 2. Of those that a mesh axis runs over, the one named last changes fastest.
Arguments:
- tokens: bfloat16 [8, 512, 2048], P('shard', 'ctx'), may hold values from -6 to 6
- cotangent: bfloat16 [8, 512, 2048], P('shard', 'ctx'), may hold values from -6 to 6
- adapter_index: int32 [8, 1], P('shard'), may hold values from 0 to 7
- w_attn: bfloat16 [4, 2048, 2048], P(None, 'shard'), may hold values from -0.125 to 0.125
- w_gate_up: bfloat16 [2, 2048, 8192], P(None, 'shard'), may hold values from -0.125 to 0.125
- w_down: bfloat16 [8192, 2048], P('shard'), may hold values from -0.0625 to 0.0625
- gains: bfloat16 [4, 2048], P(None, 'shard'), may hold values from 0.5 to 1.5
- a_wide: bfloat16 [6, 8, 16, 2048], P(None, None, None, 'shard'), may hold values from -0.125 to 0.125
- a_down: bfloat16 [8, 16, 8192], P(None, None, 'shard'), may hold values from -0.0625 to 0.0625
- b_model: bfloat16 [5, 8, 16, 2048], P(None, None, None, 'shard'), may hold values from -1.5 to 1.5
- b_hidden: bfloat16 [2, 8, 16, 8192], P(None, None, None, 'shard'), may hold values from -1.5 to 1.5
Outputs:
- output: bfloat16 [8, 512, 2048], P('shard', 'ctx')
- input_grad: float32 [8, 512, 2048], P('shard', 'ctx')
- grad_a_wide: float32 [6, 8, 16, 2048], P(None, None, None, 'shard')
- grad_a_down: float32 [8, 16, 8192], P(None, None, 'shard')
- grad_b_model: float32 [5, 8, 16, 2048], P(None, None, None, 'shard')
- grad_b_hidden: float32 [2, 8, 16, 8192], P(None, None, None, 'shard')
Inputs may be any that keep to these rules, and one draw needn't show every extreme that they name: `adapter_index`: every one of the 8 adapters is the adapter of at least one sequence.
All inputs are finite; a program needn't handle non-finite values.
Results may differ from a plain program's by a relative error of at most 0.025.
Values may be sent and summed in bfloat16 or wider, within the bound.
No kernel may reach another device: no remote copies, remote signals or barrier semaphores. Data moves between devices by JAX's collectives and lax.ppermute only.
A program may use at most 512 MiB of HBM per device.

v0:
```python
import functools
import math

import jax
import jax.numpy as jnp
from jax import lax
from jax.experimental import pallas as pl
from jax.experimental.pallas import tpu as pltpu
from jax.sharding import PartitionSpec as P

D = 2048
HEADS = 16
HD = 128
BLOCK = 256

epsilon = 1e-06
rope_base = 500000.0
far_below = -1e30
BF = jnp.bfloat16
F32 = jnp.float32
VMEM_BYTES = 16 * 2**20


def dot(left, right):
    return lax.dot_general(left, right, (((1,), (0,)), ((), ())), preferred_element_type=F32)


def dot_nt(left, right):
    return lax.dot_general(left, right, (((1,), (1,)), ((), ())), preferred_element_type=F32)


def dot_tn(left, right):
    return lax.dot_general(left, right, (((0,), (0,)), ((), ())), preferred_element_type=F32)


def over_shard(value, flip):
    size = lax.axis_size("shard")
    return lax.ppermute(value, "shard", [(i, i ^ flip) for i in range(size)])


class Windows:
    def __init__(self):
        self.carried = []

    def side_by_side(self, run, inputs, sends):
        values = [value for _, value in sends]
        inputs, values, self.carried = lax.optimization_barrier((inputs, values, self.carried))
        got = [send(value) for (send, _), value in zip(sends, values)]
        out = run(inputs) if run else None
        out, got, self.carried = lax.optimization_barrier((out, got, self.carried))
        return out, got


def over_ctx(value, flip):
    size = lax.axis_size("ctx")
    return lax.ppermute(value, "ctx", [(i, i ^ flip) for i in range(size)])


FLIPS = (0, 2, 1, 3)


def call(body, grid, args, in_specs, outs, scratch=(), scalars=(), flops=0, aliases={}):
    placed = []
    for arg, spec in zip(args, in_specs):
        if spec.memory_space == pltpu.VMEM:
            arg = pltpu.with_memory_space_constraint(arg, pltpu.VMEM)
        elif spec.memory_space == pltpu.HBM:
            arg = pltpu.with_memory_space_constraint(arg, pltpu.HBM)
        placed.append(arg)
    return pl.pallas_call(
        body,
        grid_spec=pltpu.PrefetchScalarGridSpec(
            num_scalar_prefetch=len(scalars),
            grid=grid,
            in_specs=in_specs,
            out_specs=[spec for _, spec in outs],
            scratch_shapes=scratch,
        ),
        out_shape=[shape for shape, _ in outs],
        input_output_aliases=aliases,
        compiler_params=pltpu.CompilerParams(vmem_limit_bytes=VMEM_BYTES),
        cost_estimate=pl.CostEstimate(flops=flops, bytes_accessed=0, transcendentals=0),
    )(*scalars, *placed)


def shape_of(shape, kind):
    return jax.ShapeDtypeStruct(shape, kind)


def whole(value):
    zeros = (0,) * value.ndim
    return pl.BlockSpec(value.shape, lambda *_: zeros)


def spec(block, index):
    return pl.BlockSpec(block, lambda i, *_: index(i))


def column_spec(value, tile):
    zeros = (0,) * (value.ndim - 1)
    return pl.BlockSpec(value.shape[:-1] + (tile,), lambda i, *_: (*zeros, i))


HBM = pl.BlockSpec(memory_space=pltpu.HBM)
ANY = pl.BlockSpec(memory_space=pl.ANY)
VMEM = pl.BlockSpec(memory_space=pltpu.VMEM)


def tile_of(width):
    return min(1024, width)


def run_copies(copies):
    for copy in copies:
        copy.start()
    for copy in copies:
        copy.wait()


def cut_body(first, apart, places, weight, near, *refs):
    fars, sems = refs[:-1], refs[-1]
    step = pl.program_id(0)
    width = near.shape[2]
    slim = fars[0].shape[1]
    rows = pl.ds(pl.multiple_of(places[1] * slim, slim), slim)

    def columns(flip):
        return pl.ds(pl.multiple_of((places[0] ^ flip) * width, width), width)

    def copies(far, cross):
        sources = [(slice(None), columns(1), near), (rows, columns(2), far), (rows, columns(3), cross)]
        return [
            pltpu.make_async_copy(weight.at[first + step, r, c], to.at[0], sems.at[i])
            for i, (r, c, to) in enumerate(sources)
        ]

    if apart:
        for matrix in range(len(fars) // 2):
            pair = fars[2 * matrix : 2 * matrix + 2]
            pl.when(step == matrix)(functools.partial(lambda pair: run_copies(copies(*pair)), pair))
    else:
        run_copies(copies(*fars))


def cut(weight, first, count, places, apart):
    depth, full = weight.shape[1:]
    width, slim = full // 4, depth // 4
    if apart:
        far = (shape_of((1, slim, width), BF), pl.BlockSpec((1, slim, width), lambda *_: (0, 0, 0)))
    else:
        far = (shape_of((count, slim, width), BF), pl.BlockSpec((1, slim, width), lambda m, _: (m, 0, 0)))
    return call(
        functools.partial(cut_body, first, apart),
        (count,),
        [weight],
        [HBM],
        [(shape_of((count, depth, width), BF), pl.BlockSpec((1, depth, width), lambda m, _: (m, 0, 0)))]
        + [far] * (2 * count if apart else 2),
        [pltpu.SemaphoreType.DMA((3,))],
        scalars=[places],
    )


COPIES = 10
PARTS = 8


def copies_of(weight, matrix, near, near_at, parts, at, places, held, sems):
    width = held.shape[1]
    depth = held.shape[0] // 4
    slim = depth // 4
    shard, quarter = places[0], places[1]

    def to(flip, rows, begin=0):
        start = pl.multiple_of((shard ^ flip) * depth + begin, slim)
        return held.at[pl.ds(start, rows), :]

    pairs = []
    if weight is not None:
        own_columns = pl.ds(pl.multiple_of(shard * width, width), width)
        pairs.append((weight.at[matrix, :, own_columns], to(0, depth)))
    if near is not None:
        pairs.append((near.at[near_at], to(1, depth)))
    for i, part in enumerate(parts):
        if part is not None:
            pairs.append((part.at[at], to(2 + i % 2, slim, (quarter ^ (i // 2)) * slim)))
    return [pltpu.make_async_copy(source, target, sems.at[i]) for i, (source, target) in enumerate(pairs)]


DONE = (shape_of((8, 128), F32), pl.BlockSpec((8, 128), lambda *_: (0, 0)))


def load_plain_body(attn, down, out_held, down_held, done, sems):
    run_copies(
        [
            pltpu.make_async_copy(attn.at[attn.shape[0] - 1], out_held, sems.at[0]),
            pltpu.make_async_copy(down, down_held, sems.at[1]),
        ]
    )
    done[...] = jnp.zeros_like(done)


def load_plain(w_attn, w_down):
    return call(
        load_plain_body,
        (1,),
        [w_attn, w_down],
        [HBM] * 2,
        [(pltpu.VMEM(w_attn.shape[1:], BF), VMEM), (pltpu.VMEM(w_down.shape, BF), VMEM), DONE],
        [pltpu.SemaphoreType.DMA((2,))],
    )


def load_body(first, there, places, *refs):
    refs = list(refs)
    weight, near = (refs.pop(0), refs.pop(0)) if first else (None, None)
    parts = [[refs.pop(0) if is_there else None for is_there in matrix] for matrix in there]
    held, done, sems = refs[-3:]
    copies = []
    for m, matrix_parts in enumerate(parts):
        copies += copies_of(weight, m, near, m, matrix_parts, 0, places, held.at[m], sems.at[m])
    run_copies(copies)
    done[...] = jnp.zeros_like(done)


def load(parts, places, weight=None, near=None, held=None):
    there = [[part is not None for part in matrix] for matrix in parts]
    arrays = [part for matrix in parts for part in matrix if part is not None]
    arrays = ([weight, near] if held is None else []) + arrays
    depth, full = (weight if held is None else held).shape[1:]
    shape = (2, 4 * depth, full // 4) if held is None else held.shape
    return call(
        functools.partial(load_body, held is None, there),
        (1,),
        arrays + ([] if held is None else [held]),
        ([HBM] + [ANY] * (len(arrays) - 1) if held is None else [ANY] * len(arrays) + [VMEM]),
        [(pltpu.VMEM(shape, BF), VMEM), DONE],
        [pltpu.SemaphoreType.DMA((2, COPIES))],
        [places],
        aliases={} if held is None else {1 + len(arrays): 0},
    )


def row_of(column):
    return jnp.transpose(jnp.broadcast_to(column, (column.shape[0], 128)))[:8]


def column_of(row):
    return jnp.transpose(jnp.broadcast_to(row[:1], (128, row.shape[1])))[:, :1]


def qkv_body(chunks, size, places, *refs):
    x_refs, refs = refs[:3], refs[3:]
    weight, near, weight_parts, refs = refs[0], refs[1], refs[2 : 2 + PARTS], refs[2 + PARTS :]
    down, up, pre, low, sums, kept, held, rows, sems, keep_sems = refs
    step = pl.program_id(0)

    def copies(p):
        return copies_of(weight, p, near, p, weight_parts, p, places, held.at[p], sems.at[p])

    @pl.when(step == 0)
    def _():
        for p in range(held.shape[0]):
            for copy in copies(p):
                copy.start()
        for h in range(chunks):
            rows[4 * h * size : 4 * (h + 1) * size] = load_parts(x_refs, h * size, size)

    lowrank = dot_nt(rows[...], down[...]).astype(BF)
    for copy in copies(step):
        copy.wait()
    keep = [pltpu.make_async_copy(held.at[p], kept.at[p], keep_sems.at[p]) for p in range(held.shape[0])]
    for p, copy in enumerate(keep):
        pl.when(step == p)(copy.start)
    value = dot(rows[...], held[step]) + dot(lowrank, up[0])
    pre[0] = value.astype(BF)
    low[0] = lowrank
    sums[...] = row_of(jnp.sum(value * value, axis=1, keepdims=True))

    @pl.when(step == held.shape[0] - 1)
    def _():
        for copy in keep:
            copy.wait()


def qkv_forward(x_parts, chunks, size, weight, weight_parts, places, downs, ups):
    count, depth, width = weight_parts[0].shape
    full = x_parts[0].shape[1]
    total, rank = 4 * chunks * size, ups.shape[1]
    return call(
        functools.partial(qkv_body, chunks, size),
        (count,),
        [*x_parts, weight, *weight_parts, downs, ups],
        [whole(x) for x in x_parts]
        + [HBM] * (2 + PARTS)
        + [
            spec((rank, full), lambda p: (p, 0)),
            spec((1, rank, width), lambda p: (p, 0, 0)),
        ],
        [
            (shape_of((count, total, width), BF), spec((1, total, width), lambda p: (p, 0, 0))),
            (shape_of((count, total, rank), BF), spec((1, total, rank), lambda p: (p, 0, 0))),
            (shape_of((8 * count, total), F32), spec((8, total), lambda p: (p, 0))),
            (pltpu.HBM((count, full, width), BF), HBM),
        ],
        [
            pltpu.VMEM((count, full, width), BF),
            pltpu.VMEM((total, full), BF),
            pltpu.SemaphoreType.DMA((count, COPIES)),
            pltpu.SemaphoreType.DMA((count,)),
        ],
        [places],
        flops=2 * total * full * width * count,
    )


def aligned_sums(refs, which, chunks):
    total = refs[0].shape[1]
    block = total // (4 * chunks)
    out = 0.0
    for flip, ref in zip(FLIPS, refs):
        column = column_of(ref[8 * which : 8 * which + 8])
        if flip:
            order = [FLIPS.index(f ^ flip) for f in FLIPS]
            column = jnp.concatenate(
                [
                    column[(4 * h + i) * block : (4 * h + i + 1) * block]
                    for h in range(chunks)
                    for i in order
                ]
            )
        out = out + column
    return out


def attention_body(chunks, factor, *refs):
    (
        query_pre, key_pre, value, own, far, near, cross, cosine, sine, gains,
        query_out, key_out, mixed_out, logs_out, scale_rows,
    ) = refs
    total = query_pre.shape[1]
    size = total // chunks

    @pl.when(pl.program_id(0) == 0)
    def _():
        for p in range(2):
            sums = aligned_sums((own, far, near, cross), p, chunks)
            scale_rows[p] = jnp.broadcast_to(lax.rsqrt(sums / D + epsilon), (total, HD))

    def prepared(pre, p):
        value = pre[0].astype(F32) * scale_rows[p] * gains[p : p + 1]
        return (value * cosine[...] + pltpu.roll(value, HD // 2, 1) * sine[...]).astype(BF)

    query, key = prepared(query_pre, 0), prepared(key_pre, 1)
    query_out[...] = query
    key_out[...] = key
    logs = []
    for h in range(chunks):
        seen = (h + 1) * size
        scores = dot_nt(query[h * size : (h + 1) * size], key[:seen]) * factor
        top = jnp.max(scores, axis=1, keepdims=True)
        weights = jnp.exp(scores - top)
        sums = jnp.sum(weights, axis=1, keepdims=True)
        probs = (weights * (1.0 / sums)).astype(BF)
        mixed_out[h * size : (h + 1) * size] = dot(probs, value[0, :seen]).astype(BF)
        logs.append(top + jnp.log(sums))
    logs_out[...] = row_of(jnp.concatenate(logs))


def attention_forward(pre, sums, cosine, sine, gains, chunks):
    _, total, width = pre.shape
    heads = width // HD
    factor = 1.0 / math.sqrt(HD)

    def head(p):
        return spec((1, total, HD), lambda i: (p, 0, i))

    by_head = spec((total, HD), lambda i: (0, i))
    return call(
        functools.partial(attention_body, chunks, factor),
        (heads,),
        [pre, pre, pre, *sums, cosine, sine, gains],
        [head(0), head(1), head(2)]
        + [whole(s) for s in sums]
        + [whole(cosine), whole(sine), spec((gains.shape[0], HD), lambda i: (0, i))],
        [
            (shape_of((total, width), BF), by_head),
            (shape_of((total, width), BF), by_head),
            (shape_of((total, width), BF), by_head),
            (shape_of((8 * heads, total), F32), spec((8, total), lambda i: (i, 0))),
        ],
        [pltpu.VMEM((2, total, HD), F32)],
        flops=4 * total * total * width,
    )


def attention_back_body(chunks, factor, *refs):
    (
        query_in, key_in, query_pre, key_pre, value, grad_in, logs, cosine, sine, gains,
        query_out, key_out, value_out, inner_out, inner_rows,
    ) = refs
    total = query_in.shape[0]
    size = total // chunks
    head = pl.program_id(0)
    query, key, values, grad = query_in[...], key_in[...], value[0], grad_in[...]
    log_column = column_of(logs[...])
    grad_key = [0.0] * chunks
    grad_value = [0.0] * chunks
    grad_query = []
    for h in range(chunks):
        rows = slice(h * size, (h + 1) * size)
        grad_row = 0.0
        delta = 0.0
        kept = []
        for k in range(h + 1):
            keys = slice(k * size, (k + 1) * size)
            scores = dot_nt(query[rows], key[keys]) * factor
            probs = jnp.exp(scores - log_column[rows])
            grad_probs = dot_nt(grad[rows], values[keys])
            delta = delta + jnp.sum(probs * grad_probs, axis=1, keepdims=True)
            kept.append((probs, grad_probs))
        for k, (probs, grad_probs) in enumerate(kept):
            keys = slice(k * size, (k + 1) * size)
            grad_scores = (probs * (grad_probs - delta)).astype(BF)
            grad_row = grad_row + dot(grad_scores, key[keys])
            grad_key[k] = grad_key[k] + dot_tn(grad_scores, query[rows])
            grad_value[k] = grad_value[k] + dot_tn(probs.astype(BF), grad[rows])
        grad_query.append(grad_row)

    value_out[...] = jnp.concatenate(grad_value).astype(BF)
    for p, (pre, grads, out) in enumerate(
        ((query_pre, grad_query, query_out), (key_pre, grad_key, key_out))
    ):
        turned = jnp.concatenate(grads) * factor
        turned = turned * cosine[...] - pltpu.roll(turned, HD // 2, 1) * sine[...]
        turned = turned * gains[p : p + 1]
        out[...] = turned.astype(BF)
        inner = jnp.sum(turned * pre[0].astype(F32), axis=1, keepdims=True)
        inner = jnp.broadcast_to(inner, (total, 128))

        @pl.when(head == 0)
        def _():
            inner_rows[p] = inner

        @pl.when(head > 0)
        def _():
            inner_rows[p] += inner

    @pl.when(head == pl.num_programs(0) - 1)
    def _():
        for p in range(2):
            inner_out[8 * p : 8 * p + 8] = jnp.transpose(inner_rows[p])[:8]


def attention_back(queries, key_rows, pre, grad_mixed, logs, cosine, sine, gains, chunks):
    _, total, width = pre.shape
    heads = width // HD
    factor = 1.0 / math.sqrt(HD)

    def head(p):
        return spec((1, total, HD), lambda i: (p, 0, i))

    by_head = spec((total, HD), lambda i: (0, i))
    return call(
        functools.partial(attention_back_body, chunks, factor),
        (heads,),
        [queries, key_rows, pre, pre, pre, grad_mixed, logs, cosine, sine, gains],
        [by_head, by_head, head(0), head(1), head(2), by_head]
        + [spec((8, total), lambda i: (i, 0)), whole(cosine), whole(sine)]
        + [spec((gains.shape[0], HD), lambda i: (0, i))],
        [
            (shape_of((total, width), BF), by_head),
            (shape_of((total, width), BF), by_head),
            (shape_of((total, width), BF), by_head),
            (shape_of((16, total), F32), pl.BlockSpec((16, total), lambda *_: (0, 0))),
        ],
        [pltpu.VMEM((2, total, 128), F32)],
        flops=10 * total * total * width,
    )


def split_out(value, keep, send):
    if keep.ndim == 2:
        half = value.shape[0] // 2
        keep[...] = value[:half].astype(BF)
        send[...] = value[half:].astype(BF)
        return
    half = keep.shape[1]
    for h in range(keep.shape[0]):
        keep[h] = value[2 * h * half : (2 * h + 1) * half].astype(BF)
        send[h] = value[(2 * h + 1) * half : (2 * h + 2) * half].astype(BF)


def qkv_grads_body(chunks, *refs):
    query_grad, key_grad, value_grad, query_pre, key_pre = refs[:5]
    squares, inners, x_refs = refs[5:9], refs[9:13], refs[13:16]
    low, ups, grads, lows, down_out, up_out = refs[16:]
    rank = ups.shape[1]
    total = query_grad.shape[0]
    for p, (grad, pre) in enumerate(((query_grad, query_pre), (key_grad, key_pre))):
        scale = lax.rsqrt(aligned_sums(squares, p, chunks) / D + epsilon)
        inner = aligned_sums(inners, p, chunks) * (scale * scale * scale / D)
        grads[p] = (grad[...].astype(F32) * scale - pre[0].astype(F32) * inner).astype(BF)
    grads[2] = value_grad[...]
    for p in range(3):
        lows[:, p * rank : (p + 1) * rank] = dot_nt(grads[p], ups[p]).astype(BF)
        up_out[p] = dot_tn(low[p], grads[p])
    size = total // chunks
    down = 0.0
    for h in range(chunks):
        x = load_parts(x_refs, h * size // 4, size // 4)
        down += dot_tn(lows[h * size : (h + 1) * size], x)
    down_out[...] = down


def qkv_grads(turned, grad_values, pre, squares, inners, x_parts, low, ups, chunks):
    count, total, width = pre.shape
    rank = ups.shape[1]
    full = x_parts[0].shape[1]

    def pre_rows(p):
        return pl.BlockSpec((1, total, width), lambda *_: (p, 0, 0))

    outs = [
        shape_of((count, total, width), BF),
        shape_of((total, count * rank), BF),
        shape_of((count * rank, full), F32),
        shape_of((count, rank, width), F32),
    ]
    return call(
        functools.partial(qkv_grads_body, chunks),
        (1,),
        [*turned, grad_values, pre, pre, *squares, *inners, *x_parts, low, ups],
        [whole(turned[0]), whole(turned[1]), whole(grad_values), pre_rows(0), pre_rows(1)]
        + [whole(v) for v in (*squares, *inners, *x_parts, low)]
        + [pl.BlockSpec((count, rank, width), lambda *_: (0, 0, 0))],
        [(o, whole(o)) for o in outs],
        flops=2 * total * width * 512,
    )


def qkv_back_body(grads, lows, weight, downs, keep, send):
    value = dot(lows[...], downs[...])
    for p in range(3):
        value += dot_nt(grads[p], weight[p])
    split_out(value, keep, send)


def qkv_back(grads, lows, weight, downs, chunks):
    count, full, width = weight.shape
    total = grads.shape[1]
    tile = tile_of(full)
    half = total // chunks // 2
    part = (shape_of((chunks, half, full), BF), spec((chunks, half, tile), lambda i: (0, 0, i)))
    return call(
        qkv_back_body,
        (full // tile,),
        [grads, lows, weight, downs],
        [
            whole(grads),
            whole(lows),
            spec((count, tile, width), lambda i: (0, i, 0)),
            spec((downs.shape[0], tile), lambda i: (0, i)),
        ],
        [part, part],
        flops=2 * total * full * width * count,
    )


def partial_body(streamed, beside, x, weight, down, up, *refs):
    keep, send, low, *scratch = refs[beside:]
    step = pl.program_id(0)
    tile = keep.shape[1]

    def columns(i):
        return pl.ds(pl.multiple_of(i * tile, tile), tile)

    def copy(i):
        held, sems = scratch
        return pltpu.make_async_copy(weight.at[:, columns(i)], held.at[:, columns(i)], sems.at[i])

    @pl.when(step == 0)
    def _():
        if streamed:
            for i in range(weight.shape[1] // tile):
                copy(i).start()
        low[...] = dot_nt(x[...], down[...]).astype(BF)

    if streamed:
        copy(step).wait()
        held = scratch[0]
    else:
        held = weight
    split_out(dot(x[...], held[:, columns(step)]) + dot(low[...], up[...]), keep, send)


def partial_forward(x, chunk, chunks, weight, down, up, streamed, beside=()):
    total, depth = x.shape
    size = total // chunks
    full = weight.shape[-1]
    tile = tile_of(full)
    half = size // 2
    rank = down.shape[0]
    scratch = [pltpu.VMEM(weight.shape, BF), pltpu.SemaphoreType.DMA((full // tile,))]
    return call(
        functools.partial(partial_body, streamed, len(beside)),
        (full // tile,),
        [x, weight, down, up, *beside],
        [
            pl.BlockSpec((size, depth), lambda *_: (chunk, 0)),
            HBM if streamed else VMEM,
            whole(down),
            spec((rank, tile), lambda i: (0, i)),
            *[VMEM] * len(beside),
        ],
        [
            (shape_of((half, full), BF), spec((half, tile), lambda i: (0, i))),
            (shape_of((half, full), BF), spec((half, tile), lambda i: (0, i))),
            (shape_of((size, rank), BF), pl.BlockSpec((size, rank), lambda *_: (0, 0))),
        ],
        scratch if streamed else (),
        flops=2 * size * depth * full,
    )


def gate_up_body(*refs):
    x_refs, (weight, downs, ups, gate, upper, act, low, rows) = refs[:4], refs[4:]
    rank = ups.shape[1]
    tile = gate.shape[1]
    step = pl.program_id(0)

    @pl.when(step == 0)
    def _():
        rows[...] = load_parts(x_refs)
        low[...] = dot_nt(rows[...], downs[...]).astype(BF)

    columns = pl.ds(pl.multiple_of(step * tile, tile), tile)
    gate_pre = dot(rows[...], weight[0, :, columns]) + dot(low[:, :rank], ups[0])
    upper_pre = dot(rows[...], weight[1, :, columns]) + dot(low[:, rank:], ups[1])
    gate[...] = gate_pre.astype(BF)
    upper[...] = upper_pre.astype(BF)
    act[...] = (gate_pre * jax.nn.sigmoid(gate_pre) * upper_pre).astype(BF)


def gate_up_forward(x_parts, weight, downs, ups):
    _, full, width = weight.shape
    size = 4 * x_parts[0].shape[0]
    rank = ups.shape[1]
    tile = tile_of(width)
    out = (shape_of((size, width), BF), spec((size, tile), lambda i: (0, i)))
    return call(
        gate_up_body,
        (width // tile,),
        [*x_parts, weight, downs, ups],
        [whole(x) for x in x_parts] + [VMEM, whole(downs), spec((2, rank, tile), lambda i: (0, 0, i))],
        [
            out,
            out,
            out,
            (shape_of((size, 2 * rank), BF), pl.BlockSpec((size, 2 * rank), lambda *_: (0, 0))),
        ],
        [pltpu.VMEM((size, full), BF)],
        flops=4 * size * full * width,
    )


def feed_back_body(*refs):
    g_refs = refs[:4]
    weight, down, gate, upper, gate_low, feed_low, feed_up, ups, _ = refs[4:13]
    gate_grad, upper_grad, low_out, down_a, feed_b, hidden_b, rows, low, lows = refs[13:]
    rank = down.shape[0]
    step = pl.program_id(0)
    @pl.when(step == 0)
    def _():
        rows[...] = load_parts(g_refs)
        low[...] = dot_nt(rows[...], feed_up[...]).astype(BF)
        feed_b[...] = dot_tn(feed_low[...], rows[...])
        lows[...] = jnp.zeros_like(lows)

    tile = gate.shape[1]
    held_rows = pl.ds(pl.multiple_of(step * tile, tile), tile)
    grad_act = dot_nt(rows[...], weight[held_rows]) + dot(low[...], down[...])
    gate_pre, upper_pre = gate[...].astype(F32), upper[...].astype(F32)
    sig = jax.nn.sigmoid(gate_pre)
    silu = gate_pre * sig
    down_a[...] = dot_tn(low[...], (silu * upper_pre).astype(BF))
    grad_upper = (grad_act * silu).astype(BF)
    grad_gate = (grad_act * upper_pre * (sig + silu * (1.0 - sig))).astype(BF)
    gate_grad[...] = grad_gate
    upper_grad[...] = grad_upper
    hidden_b[0] = dot_tn(gate_low[:, :rank], grad_gate)
    hidden_b[1] = dot_tn(gate_low[:, rank:], grad_upper)
    lows[:, :rank] += dot_nt(grad_gate, ups[0])
    lows[:, rank:] += dot_nt(grad_upper, ups[1])

    @pl.when(step == pl.num_programs(0) - 1)
    def _():
        low_out[...] = lows[...].astype(BF)


def feed_back(g_parts, weight, down, gate, upper, gate_low, feed_low, feed_up, ups, beside):
    width, depth = weight.shape
    size = 4 * g_parts[0].shape[0]
    rank = down.shape[0]
    tile = tile_of(width)
    by_tile = spec((size, tile), lambda i: (0, i))
    return call(
        feed_back_body,
        (width // tile,),
        [*g_parts, weight, down, gate, upper, gate_low, feed_low, feed_up, ups, beside],
        [whole(g) for g in g_parts]
        + [
            VMEM,
            spec((rank, tile), lambda i: (0, i)),
            by_tile,
            by_tile,
            whole(gate_low),
            whole(feed_low),
            whole(feed_up),
            spec((2, rank, tile), lambda i: (0, 0, i)),
            VMEM,
        ],
        [
            (shape_of((size, width), BF), by_tile),
            (shape_of((size, width), BF), by_tile),
            (shape_of((size, 2 * rank), BF), pl.BlockSpec((size, 2 * rank), lambda *_: (0, 0))),
            (shape_of((rank, width), F32), spec((rank, tile), lambda i: (0, i))),
            (shape_of((rank, depth), F32), pl.BlockSpec((rank, depth), lambda *_: (0, 0))),
            (shape_of((2, rank, width), F32), spec((2, rank, tile), lambda i: (0, 0, i))),
        ],
        [
            pltpu.VMEM((size, depth), BF),
            pltpu.VMEM((size, rank), BF),
            pltpu.VMEM((size, 2 * rank), F32),
        ],
        flops=2 * size * depth * width,
    )


def gate_up_back_body(gate_grad, upper_grad, weight, low, downs, *refs):
    x_refs, (keep, send, down_out) = refs[:4], refs[4:]
    tile = keep.shape[1]
    held_rows = pl.ds(pl.multiple_of(pl.program_id(0) * tile, tile), tile)
    value = dot_nt(gate_grad[...], weight[0, held_rows]) + dot_nt(upper_grad[...], weight[1, held_rows])
    split_out(value + dot(low[...], downs[...]), keep, send)
    down_out[...] = dot_tn(low[...], load_parts(x_refs))


def gate_up_back(gate_grad, upper_grad, weight, low, downs, x_parts):
    _, full, width = weight.shape
    size = gate_grad.shape[0]
    half = size // 2
    ranks = downs.shape[0]
    tile = tile_of(full)
    return call(
        gate_up_back_body,
        (full // tile,),
        [gate_grad, upper_grad, weight, low, downs, *x_parts],
        [whole(gate_grad), whole(upper_grad), VMEM, whole(low), spec((ranks, tile), lambda i: (0, i))]
        + [column_spec(x, tile) for x in x_parts],
        [
            (shape_of((half, full), BF), spec((half, tile), lambda i: (0, i))),
            (shape_of((half, full), BF), spec((half, tile), lambda i: (0, i))),
            (shape_of((ranks, full), F32), spec((ranks, tile), lambda i: (0, i))),
        ],
        flops=4 * size * full * width,
    )


def out_back_body(*refs):
    g_refs = refs[:4]
    weight, down, up, mixed, low, grad_mixed, down_out, up_out, rows, grad_low = refs[4:]

    @pl.when(pl.program_id(0) == 0)
    def _():
        rows[...] = load_parts(g_refs)
        grad_low[...] = dot_nt(rows[...], up[...]).astype(BF)
        up_out[...] = dot_tn(low[...], rows[...])

    tile = grad_mixed.shape[1]
    held_rows = pl.ds(pl.multiple_of(pl.program_id(0) * tile, tile), tile)
    grad_mixed[...] = (dot_nt(rows[...], weight[held_rows]) + dot(grad_low[...], down[...])).astype(BF)
    down_out[...] = dot_tn(grad_low[...], mixed[...])


def out_back(g_parts, weight, down, up, mixed, low, chunk):
    width, depth = weight.shape
    size = 4 * g_parts[0].shape[0]
    rank = down.shape[0]
    tile = min(256, width)
    return call(
        out_back_body,
        (width // tile,),
        [*g_parts, weight, down, up, mixed, low],
        [whole(g) for g in g_parts]
        + [
            VMEM,
            spec((rank, tile), lambda i: (0, i)),
            whole(up),
            spec((size, tile), lambda i: (chunk, i)),
            whole(low),
        ],
        [
            (shape_of((size, width), BF), spec((size, tile), lambda i: (0, i))),
            (shape_of((rank, width), F32), spec((rank, tile), lambda i: (0, i))),
            (shape_of((rank, depth), F32), pl.BlockSpec((rank, depth), lambda *_: (0, 0))),
        ],
        [pltpu.VMEM((size, depth), BF), pltpu.VMEM((size, rank), BF)],
        flops=2 * size * depth * width,
    )


def load_parts(refs, first=0, count=None, columns=slice(None)):
    own, far, *near = refs
    if len(near) == 1:
        near = near[0].at[0], near[0].at[1]
    rows = slice(first, own.shape[0] if count is None else first + count)
    return jnp.concatenate([ref[rows, columns] for ref in (own, far, *near)])


def ctx_flips():
    size = lax.axis_size("ctx")
    return [flip for flip in (2, 4, 8, 16, 1) if flip < size]


def ctx_step(at):
    return lambda value: over_ctx(value, ctx_flips()[at])


def gathered_place(ctx, other):
    place = 0
    for at, flip in enumerate(ctx_flips()):
        place = place + (((ctx ^ other) // flip) % 2) * 2**at
    return place


def column_cuts(partial, starts):
    width = partial.shape[-1] // 4
    zero = jnp.uint32(0)
    blocks = [lax.dynamic_slice(partial, (zero, start), (partial.shape[0], width)) for start in starts]
    return blocks[0], blocks[1], jnp.stack(blocks[2:]).astype(BF)


def natural(parts, shard):
    out = []
    for index in range(4):
        value = parts[0]
        for flip, part in zip(FLIPS[1:], parts[1:]):
            value = jnp.where((shard ^ flip) == index, part, value)
        out.append(value)
    return out


def row_sum(keep, near, got):
    rows = got.shape[-2]
    own = (slice(None),) * (len(keep.shape) - 2) + (slice(0, rows),)
    return keep[own].astype(F32) + near[own].astype(F32) + got[...].astype(F32)


def rms_scale(value):
    return lax.rsqrt(jnp.mean(value * value, axis=-1, keepdims=True) + epsilon)


def rms_back(value, scale, gain, grad):
    weighted = grad * gain
    return scale * weighted - value * (
        scale * scale * scale * jnp.mean(value * weighted, axis=-1, keepdims=True)
    )


def far_body(keep, near, far):
    rows = far.shape[-2]
    below = (slice(None),) * (len(keep.shape) - 2) + (slice(rows, 2 * rows),)
    far[...] = (keep[below].astype(F32) + near[below].astype(F32)).astype(BF)


def attention_rows_body(keep, near, got, token, gain, value_out, resid_out, low_out):
    value = row_sum(keep, near, got)
    resid = token[...].astype(F32) + value * rms_scale(value) * gain[...]
    value_out[...] = value
    resid_out[...] = resid
    low_out[...] = resid.astype(BF)


def feed_rows_body(keep, near, got, resid, cot, gain, output, grad):
    value = row_sum(keep, near, got)
    scale = rms_scale(value)
    output[...] = (resid[...] + value * scale * gain[...]).astype(BF)
    grad[...] = rms_back(value, scale, gain[...], cot[...].astype(F32)).astype(BF)


def back_rows_body(keep, near, got, value, cot, gain, grad_out, low_out):
    grad = cot[...].astype(F32) + row_sum(keep, near, got)
    grad_out[...] = grad
    value = value[...]
    low_out[...] = rms_back(value, rms_scale(value), gain[...], grad).astype(BF)


def far_two_body(keep, near, *fars):
    for h, far in enumerate(fars):
        far_body(keep.at[h], near.at[h], far)


def input_rows_body(order, keep, near, *refs):
    chunks = keep.shape[0]
    gots, resids, outs = refs[:chunks], refs[chunks : 2 * chunks], refs[2 * chunks :]
    rows = [
        (row_sum(keep.at[h], near.at[h], gots[h]) + resids[h][...]).astype(BF) for h in range(chunks)
    ]

    @pl.when(order[0] == 0)
    def _():
        for out, row in zip(outs, rows):
            out[...] = row

    @pl.when(order[0] != 0)
    def _():
        for out, row in zip(outs, rows[::-1]):
            out[...] = row


def input_rows(keep, near, gots, resids, order):
    args = [keep, near, *gots, *resids]
    outs = [shape_of(resid.shape, BF) for resid in resids]
    return call(
        input_rows_body, (1,), args, [whole(x) for x in args], [(o, whole(o)) for o in outs], scalars=[order]
    )


def by_rows(body, args, kinds):
    *lead, rows, width = args[0].shape
    outs = [shape_of((*lead, rows // 2, width), kind) for kind in kinds]
    return call(body, (1,), args, [whole(x) for x in args], [(o, whole(o)) for o in outs])


def rotate(value, cosine, sine):
    half = value.shape[-1] // 2
    turned = jnp.concatenate([value[..., half:], value[..., :half]], axis=-1)
    return value * cosine[:, None, :] + turned * sine[:, None, :]


def realign(value, flip, chunks):
    shape = value.shape
    value = value.reshape(shape[0], chunks, 2, 2, -1)
    if flip & 1:
        value = value[:, :, ::-1]
    if flip & 2:
        value = value[:, :, :, ::-1]
    return value.reshape(shape)


def group_of(sequence, part, per_sequence, ctx_size):
    if per_sequence > 1:
        return sequence * per_sequence + part
    depth = sequence % (ctx_size // 2)
    return 2 * depth + (depth + sequence // (ctx_size // 2)) % 2


def sequence_of(ctx, per_sequence, ctx_size):
    if per_sequence > 1:
        return ctx // per_sequence, ctx % per_sequence
    depth = ctx // 2
    return depth + ctx_size // 2 * ((ctx + depth) % 2), 0 * ctx


def wide_attention(pre, sums, cosine, sine, gains, chunks, positions, groups):
    _, total, width = pre.shape
    heads = width // HD
    pre = pre.astype(F32)
    squares = sum(realign(s[::8], flip, chunks) for flip, s in zip(FLIPS, sums))
    scales = lax.rsqrt(squares[:2] / D + epsilon)[:, :, None]

    def as_heads(value):
        return value.reshape(total, heads, HD)

    queries, key_rows = [
        rotate(as_heads(pre[p] * scales[p] * gains[p]), cosine, sine).astype(BF) for p in range(2)
    ]

    def over_sequence(value):
        return lax.all_gather(value, "ctx", axis=0, tiled=True, axis_index_groups=groups)

    key_all, value_all = over_sequence(key_rows), over_sequence(as_heads(pre[2].astype(BF)))
    visible = over_sequence(positions // BLOCK)[None, :] <= (positions // BLOCK)[:, None]
    factor = 1.0 / math.sqrt(HD)
    scores = jnp.einsum("qhd,khd->hqk", queries, key_all, preferred_element_type=F32) * factor
    scores = jnp.where(visible, scores, far_below)
    weights = jnp.exp(scores - jnp.max(scores, axis=-1, keepdims=True))
    probs = weights / jnp.sum(weights, axis=-1, keepdims=True)
    mixed = jnp.einsum("hqk,khd->qhd", probs.astype(BF), value_all, preferred_element_type=F32)
    mixed = mixed.astype(BF).reshape(total, width)

    def back(grad_mixed):
        grad = as_heads(grad_mixed)
        grad_probs = jnp.einsum("qhd,khd->hqk", grad, value_all, preferred_element_type=F32)
        delta = jnp.sum(probs * grad_probs, axis=-1, keepdims=True)
        grad_scores = (probs * (grad_probs - delta)).astype(BF)
        grad_queries = jnp.einsum("hqk,khd->qhd", grad_scores, key_all, preferred_element_type=F32)
        grad_keys = jnp.einsum("hqk,qhd->khd", grad_scores, queries, preferred_element_type=F32)
        grad_values = jnp.einsum("hqk,qhd->khd", probs.astype(BF), grad, preferred_element_type=F32)
        grad_keys, grad_values = [
            lax.psum_scatter(
                g.astype(BF), "ctx", scatter_dimension=0, tiled=True, axis_index_groups=groups
            ).astype(F32)
            for g in (grad_keys * factor, grad_values)
        ]
        turned = [
            rotate(g, cosine, -sine).reshape(total, width) * gains[p]
            for p, g in enumerate((grad_queries * factor, grad_keys))
        ]
        inner = jnp.stack([jnp.sum(turned[p] * pre[p], axis=-1) for p in range(2)])
        inner = jnp.repeat(inner, 8, axis=0)
        values = grad_values.reshape(total, width).astype(BF)
        return turned[0].astype(BF), turned[1].astype(BF), values, inner

    return mixed, back


def choose_body(place, wide, down, model, hidden, gains, wide_out, down_out, model_out, hidden_out, small, sems):
    at = place[0]
    sources = [(wide.at[:, at], wide_out), (down.at[at], down_out)]
    sources += [(model.at[:, at], model_out), (hidden.at[:, at], hidden_out)]
    run_copies([pltpu.make_async_copy(source, to, sems.at[i]) for i, (source, to) in enumerate(sources)])
    rank, width = wide_out.shape[1:]
    shared = [wide_out[p] for p in (0, 1, 2, 4, 5)] + [model_out[p] for p in (3, 4)]
    last = jnp.concatenate([gains[2:], jnp.zeros((rank - 2, width), BF)])
    for at, value in enumerate([*shared, last]):
        column = at // 2 * width
        small[at % 2 * rank : (at % 2 + 1) * rank, column : column + width] = value


def choose(place, a_wide, a_down, b_model, b_hidden, gains):
    rank, width = a_wide.shape[2:]
    shapes = [a_wide.shape[:1] + a_wide.shape[2:], a_down.shape[1:]]
    shapes += [b_model.shape[:1] + b_model.shape[2:], b_hidden.shape[:1] + b_hidden.shape[2:]]
    shapes.append((2 * rank, 4 * width))
    outs = [shape_of(s, BF) for s in shapes]
    return call(
        choose_body,
        (1,),
        [a_wide, a_down, b_model, b_hidden, gains],
        [HBM] * 4 + [whole(gains)],
        [(o, whole(o)) for o in outs],
        [pltpu.SemaphoreType.DMA((4,))],
        scalars=[place],
    )


def place_body(rank, count, unused, plan, at, *refs):
    sources, outs = refs[:count], refs[count + unused :]
    for out, maps in zip(outs, plan):
        for n in range(out.shape[1]):
            for p, pieces in enumerate(maps):
                begin = 0
                for source, place in pieces:
                    value = sources[source][at[n], place * rank : (place + 1) * rank].astype(F32)
                    out[p, n, :, begin : begin + value.shape[-1]] = value
                    begin += value.shape[-1]


def on_device(
    tokens,
    cotangent,
    adapter_index,
    w_attn,
    w_gate_up,
    w_down,
    gains,
    a_wide,
    a_down,
    b_model,
    b_hidden,
):
    seqs, rows = tokens.shape[0], tokens.shape[1]
    shards, ctxs = lax.axis_size("shard"), lax.axis_size("ctx")
    shard, ctx = lax.axis_index("shard"), lax.axis_index("ctx")
    batch = seqs * shards
    per_sequence = ctxs // batch
    group_rows = batch * rows
    chunks = seqs
    chunk_rows = shards * rows
    wide = HEADS // shards * HD
    adapters, rank = a_down.shape[:2]

    groups = [[group_of(q, k, per_sequence, ctxs) for k in range(per_sequence)] for q in range(batch)]
    my_sequence, my_part = sequence_of(ctx, per_sequence, ctxs)
    my_slot = my_sequence % seqs
    my_spot = (ctx % batch) // shards

    pairs = []
    for p in range(seqs):
        pairs.append([])
        for c in range(ctxs):
            for s in range(shards):
                k, local = c // batch, c % batch
                spot, owner = local // shards, local % shards
                to = groups[seqs * s + (p + spot) % seqs][k]
                pairs[p].append((c * shards + s, to * shards + owner))

    windows = Windows()
    side_by_side = windows.side_by_side

    def is_place(index):
        return [index % seqs == at for at in range(1, seqs)]

    flags = {
        "cut": [((p + my_spot) % seqs).astype(jnp.uint32) for p in range(seqs)],
        "chunk": [is_place(my_slot - h) for h in range(seqs)],
        "return": [is_place(my_slot - p) for p in range(seqs)],
        "order": [is_place(j - my_spot) for j in range(seqs)],
        "columns": [((shard ^ flip) * wide).astype(jnp.uint32) for flip in FLIPS],
        "places": jnp.stack([shard, ctx % 4]).astype(jnp.int32),
        "turn": [((my_slot - p) % seqs)[None].astype(jnp.int32) for p in range(seqs)],
    }

    def pick(parts, is_it):
        value = parts[0]
        for part, flag in zip(parts[1:], is_it):
            value = jnp.where(flag, part, value)
        return value

    def cut_rows(*values):
        return [
            jnp.concatenate(
                [
                    lax.dynamic_index_in_dim(value, flags["cut"][p], 0, keepdims=False)
                    for value in values
                ]
            )
            for p in range(seqs)
        ]

    def send_row(p):
        return lambda cut: lax.ppermute(cut, ("ctx", "shard"), pairs[p])

    def chunk_order(got):
        return [pick(got, flags["chunk"][h]) for h in range(seqs)]

    def return_cuts(parts):
        return [pick(parts, flags["return"][p]) for p in range(seqs)]

    def return_row(p):
        return lambda cut: lax.ppermute(cut, ("ctx", "shard"), [(b, a) for a, b in pairs[p]])

    def return_order(got):
        return jnp.stack([pick(got, flags["order"][j]) for j in range(seqs)])

    def core(value):
        return over_shard(value, 1)

    def chip(value):
        return over_shard(value, 2)

    def across(value):
        return over_shard(value, 3)

    def by_x(value):
        return over_ctx(value, 1)

    def by_z(value):
        return over_ctx(value, 2)

    def to_all(value):
        return [(functools.partial(over_shard, flip=flip), value) for flip in FLIPS[1:]]

    index_own = adapter_index[:, 0]
    (qkv_near, qkv_far, qkv_cross, flags), index_got = side_by_side(
        lambda x: (*cut(x[0], 0, 3, x[1]["places"], False), x[1]), [w_attn, flags], to_all(index_own)
    )
    places = flags["places"]
    index_all = jnp.concatenate(natural([index_own, *index_got], shard))
    sequence_with = jnp.sum(
        jnp.where(
            index_all[None, :] == jnp.arange(adapters, dtype=jnp.int32)[:, None],
            jnp.arange(batch, dtype=jnp.int32)[None, :],
            0,
        ),
        axis=1,
    )
    table = jnp.array(groups, jnp.int32)
    if per_sequence > 1:
        where = sequence_with
    else:
        group_with = jnp.sum(
            jnp.where(
                sequence_with[:, None] == jnp.arange(batch, dtype=jnp.int32)[None, :], table[:, 0][None, :], 0
            ),
            axis=1,
        )
        where = gathered_place(ctx, group_with)

    row_cuts = cut_rows(tokens)

    def rope_tables(place):
        shape = (chunks, shards, rows, HD)
        spot, turn, row, lane = [lax.broadcasted_iota(jnp.int32, shape, axis) for axis in range(4)]
        owner = place ^ (turn // 2 + turn % 2 * 2)
        position = my_part * group_rows + (spot * shards + owner) * rows + row
        freqs = jnp.exp((lane % (HD // 2)).astype(F32) * (-2.0 * math.log(rope_base) / HD))
        angles = position.astype(F32) * freqs
        sine = jnp.sin(angles) * jnp.where(lane < HD // 2, -1.0, 1.0)
        return position[..., 0].reshape(-1), jnp.cos(angles).reshape(-1, HD), sine.reshape(-1, HD)

    def prepare(x):
        chosen = choose(x[0], a_wide, a_down, b_model, b_hidden, gains)
        return chosen, cut(x[1], 0, 2, x[2], True), x[3], rope_tables(x[2][0])

    (chosen, gate_up_cuts, where, (positions, cosine, sine)), [qkv_a, qkv_b, *row_got, qkv_near] = side_by_side(
        prepare,
        [index_all[my_sequence][None], w_gate_up, places, where],
        [
            (chip, qkv_far),
            (across, qkv_cross),
            (send_row(0), row_cuts[0]),
            (send_row(1), row_cuts[1]),
            (core, qkv_near),
        ],
    )
    own_wide, own_down, own_model, own_hidden, small = chosen
    near, gate_far, gate_cross, up_far, up_cross = gate_up_cuts

    token_rows = chunk_order(row_got)
    token_own = jnp.concatenate([*token_rows, small])
    held = {}

    def load_out(weights):
        held["out"], held["down"], done = load_plain(*weights)
        return done

    done, [qkv_xa, qkv_xb, qkv_za, qkv_zb, token_far] = side_by_side(
        load_out,
        [w_attn, w_down],
        [(by_x, qkv_a), (by_x, qkv_b), (by_z, qkv_a), (by_z, qkv_b), (chip, token_own)],
    )
    windows.carried.append(done)
    _, [last_a, last_b, token_near, gate_a] = side_by_side(
        None,
        None,
        [
            (by_x, qkv_za),
            (by_z, qkv_xb),
            (core, jnp.stack([token_own, token_far])),
            (chip, gate_far),
        ],
    )
    w_qkv = [qkv_near, qkv_a, qkv_b, qkv_xa, qkv_xb, qkv_za, qkv_zb, last_a, last_b]
    token_parts = [token_own, token_far, token_near]
    small_parts = [part[..., seqs * rows :, :] for part in token_parts]
    small_parts = [small_parts[0], small_parts[1], small_parts[2][0], small_parts[2][1]]
    small_all = jnp.concatenate(
        natural(
            [
                jnp.concatenate([part[:, at * wide : (at + 1) * wide] for at in range(4)])
                for part in small_parts
            ],
            shard,
        ),
        axis=1,
    )
    qkv_downs = small_all[: 3 * rank]
    gate_downs = small_all[3 * rank : 5 * rank]
    out_up = small_all[5 * rank : 6 * rank]
    feed_up = small_all[6 * rank : 7 * rank]
    attn_gain = small_all[7 * rank : 7 * rank + 1].astype(F32)
    feed_gain = small_all[7 * rank + 1 : 7 * rank + 2].astype(F32)
    head_gains = gains[:2].astype(F32)

    (pre, qkv_low, squares, qkv_held), [gate_b, gate_xa, gate_za, near] = side_by_side(
        lambda x: qkv_forward(x, chunks, rows, w_attn, w_qkv, places, qkv_downs, own_model),
        token_parts,
        [(across, gate_cross), (by_x, gate_a), (by_z, gate_a), (core, near)],
    )

    def from_all(sums, others):
        _, got = side_by_side(None, None, to_all(sums) + others)
        return [sums, *got[:3]], got[3:]

    squares, _ = from_all(squares[:16], [])
    simple = per_sequence == 1 and chunk_rows == BLOCK
    attention_sends = [(chip, up_far), (by_x, gate_b), (by_z, gate_b)]
    if simple:
        (queries, key_rows, mixed, logs), got = side_by_side(
            lambda x: attention_forward(x[0], x[1], x[2], x[3], head_gains, chunks),
            [pre, squares, cosine, sine],
            attention_sends,
        )
    else:
        mixed, attention_grads = wide_attention(
            pre, squares, cosine, sine, head_gains, chunks, positions, groups
        )
        got = [send(value) for send, value in attention_sends]
    up_a, gate_xb, gate_zb = got

    every = range(chunks)
    assert chunks == 2
    def far_sum(keep, near):
        return by_rows(far_body, [keep, near], [BF])[0]

    def project_out(x, h):
        return partial_forward(x, h, chunks, held["out"], own_wide[3], out_up, False)

    def attention_rows(h, keep, near, got):
        return by_rows(attention_rows_body, [keep, near, got, token_rows[h], attn_gain], [F32, F32, BF])

    def feed_rows(h, keep, near, got):
        return by_rows(feed_rows_body, [keep, near, got, resid[h], cot[h], feed_gain], [BF, BF])

    def back_rows(h, keep, near, got):
        return by_rows(back_rows_body, [keep, near, got, attn_pre[h], cot[h], attn_gain], [F32, BF])

    def up_gate(parts):
        return gate_up_forward(parts, gate_up_held, gate_downs, own_hidden)

    def down(act):
        return partial_forward(act, 0, 1, held["down"], own_down, feed_up, False, [gate_up_held])

    def back_down(h, parts):
        return feed_back(
            parts, held["down"], own_down, hidden[h][0], hidden[h][1], hidden[h][3], feed_parts[h][2], feed_up, own_hidden, gate_up_held
        )

    def back_up_gate(h, gate_grad, upper_grad):
        return gate_up_back(
            gate_grad, upper_grad, gate_up_held, hidden_grads[h][2], gate_downs, resid_parts[h]
        )

    def back_out(h, parts):
        return out_back(parts, held["out"], own_wide[3], out_up, mixed, out_parts[h][2], h)

    none = [None] * PARTS

    def load_first(x):
        gate = [*x, None, None]
        held["gate_up"], done = load([gate, none], places, w_gate_up, near)
        return done

    def load_more(x):
        gate = none[:6] + x[:2]
        up = [*x[2:], None, None]
        held["gate_up"], done = load([gate, up], places, held=held["gate_up"])
        return done

    def load_last(x):
        held["gate_up"], done = load([none, none[:6] + x], places, held=held["gate_up"])
        return done

    attn_pre, resid, resid_low = [None] * 2, [None] * 2, [None] * 2
    resid_parts, hidden, feed_parts, output = [None] * 2, [None] * 2, [None] * 2, [None] * 2
    hidden_grads, resid_grads, grad_resid, out_grads = [None] * 2, [None] * 2, [None] * 2, [None] * 2
    out_parts, [up_b, up_xa, up_za] = side_by_side(
        lambda x: [project_out(x, h) for h in every], mixed, [(across, up_cross), (by_x, up_a), (by_z, up_a)]
    )
    _, [core0, core1] = side_by_side(None, None, [(core, out_parts[0][1]), (core, out_parts[1][1])])
    far0, far1 = far_sum(out_parts[0][0], core0), far_sum(out_parts[1][0], core1)
    done, [got0, got1, gate_last_a, gate_last_b] = side_by_side(
        load_first,
        [gate_a, gate_b, gate_xa, gate_xb, gate_za, gate_zb],
        [(chip, far0), (chip, far1), (by_x, gate_za), (by_z, gate_xb)],
    )
    windows.carried.append(done)
    attn_pre[0], resid[0], resid_low[0] = attention_rows(0, out_parts[0][0], core0, got0)
    attn_pre[1], resid[1], resid_low[1] = attention_rows(1, out_parts[1][0], core1, got1)
    _, [far0, near0, up_xb, up_zb] = side_by_side(
        None, None, [(chip, resid_low[0]), (core, resid_low[0]), (by_x, up_b), (by_z, up_b)]
    )
    done, [cross0, far1, near1, up_last_a, up_last_b] = side_by_side(
        load_more,
        [gate_last_a, gate_last_b, up_a, up_b, up_xa, up_xb, up_za, up_zb],
        [(core, far0), (chip, resid_low[1]), (core, resid_low[1]), (by_x, up_za), (by_z, up_xb)],
    )
    windows.carried.append(done)
    resid_parts[0] = [resid_low[0], far0, near0, cross0]
    done, [cross1] = side_by_side(load_last, [up_last_a, up_last_b], [(core, far1)])
    windows.carried.append(done)
    gate_up_held = held["gate_up"]
    resid_parts[1] = [resid_low[1], far1, near1, cross1]

    cot_cuts = cut_rows(cotangent)
    hidden[0], [cot0] = side_by_side(up_gate, resid_parts[0], [(send_row(0), cot_cuts[0])])
    feed_parts[0], _ = side_by_side(down, hidden[0][2], [])
    _, [core0] = side_by_side(None, None, [(core, feed_parts[0][1])])
    hidden[1], [got, cot1] = side_by_side(
        up_gate, resid_parts[1], [(chip, far_sum(feed_parts[0][0], core0)), (send_row(1), cot_cuts[1])]
    )
    cot = chunk_order([cot0, cot1])
    output[0], grad0 = feed_rows(0, feed_parts[0][0], core0, got)
    feed_parts[1], [far, near] = side_by_side(down, hidden[1][2], [(chip, grad0), (core, grad0)])
    _, [cross, core1] = side_by_side(None, None, [(core, far), (core, feed_parts[1][1])])
    hidden_grads[0], [got] = side_by_side(
        lambda x: back_down(0, x), [grad0, far, near, cross], [(chip, far_sum(feed_parts[1][0], core1))]
    )
    output[1], grad1 = feed_rows(1, feed_parts[1][0], core1, got)
    output = return_cuts(output)
    resid_grads[0], [far, near, output0] = side_by_side(
        lambda x: back_up_gate(0, *x),
        hidden_grads[0][:2],
        [(chip, grad1), (core, grad1), (return_row(0), output[0])],
    )
    _, [cross, core0] = side_by_side(None, None, [(core, far), (core, resid_grads[0][1])])
    hidden_grads[1], [got, output1] = side_by_side(
        lambda x: back_down(1, x),
        [grad1, far, near, cross],
        [(chip, far_sum(resid_grads[0][0], core0)), (return_row(1), output[1])],
    )
    output = return_order([output0, output1])
    grad_resid[0], grad0 = back_rows(0, resid_grads[0][0], core0, got)

    broad = jnp.concatenate(
        [sum(g[3] for g in hidden_grads), sum(g[5] for g in hidden_grads).reshape(2 * rank, -1)]
    ).astype(BF)
    broad = [x[None] for x in jnp.split(broad, 2, axis=1)]
    step0, step1, step2 = [ctx_step(at) for at in range(3)]

    def grown(value, got):
        return jnp.concatenate([value, got])

    resid_grads[1], [far, near, *got] = side_by_side(
        lambda x: back_up_gate(1, *x),
        hidden_grads[1][:2],
        [(chip, grad0), (core, grad0), (step0, broad[0]), (step0, broad[1])],
    )
    broad = [grown(*pair) for pair in zip(broad, got)]
    own_early, far_early, cuts = column_cuts(
        jnp.concatenate([sum(g[4] for g in hidden_grads), sum(g[2] for g in resid_grads)]), flags["columns"]
    )
    _, [cross, core1, got_early] = side_by_side(
        None, None, [(core, far), (core, resid_grads[1][1]), (core, cuts)]
    )
    own_early = own_early + got_early[0].astype(F32)
    far_early = (far_early + got_early[1].astype(F32)).astype(BF)
    out_grads[0], [got1, got_early, got] = side_by_side(
        lambda x: back_out(0, x),
        [grad0, far, near, cross],
        [(chip, far_sum(resid_grads[1][0], core1)), (chip, far_early), (step1, broad[0])],
    )
    broad[0] = grown(broad[0], got)
    early = (own_early + got_early.astype(F32)).astype(BF)[None]
    grad_resid[1], grad1 = back_rows(1, resid_grads[1][0], core1, got1)
    _, [far, near, got, got_early] = side_by_side(
        None, None, [(chip, grad1), (core, grad1), (step2, broad[0]), (step0, early)]
    )
    broad[0] = grown(broad[0], got)
    early = grown(early, got_early)
    _, [cross] = side_by_side(None, None, [(core, far)])
    out_grads[1] = back_out(1, [grad1, far, near, cross])
    grad_mixed = jnp.concatenate([g[0] for g in out_grads])

    attention_sends = [(step1, broad[1])]
    if simple:
        (query_turned, key_turned, grad_values, inner), [got] = side_by_side(
            lambda x: attention_back(
                queries, key_rows, pre, x, logs, cosine, sine, head_gains, chunks
            ),
            grad_mixed,
            attention_sends,
        )
    else:
        query_turned, key_turned, grad_values, inner = attention_grads(grad_mixed)
        [got] = [send(value) for send, value in attention_sends]
    broad[1] = grown(broad[1], got)
    inners, _ = from_all(inner, [])
    grads, lows, down_late, up_late = qkv_grads(
        [query_turned, key_turned], grad_values, pre, squares, inners, token_parts, qkv_low, own_model, chunks
    )
    partial = jnp.concatenate([down_late, sum(g[2] for g in out_grads)])
    cuts = [lax.dynamic_slice(partial, (jnp.uint32(0), start), (partial.shape[0], wide)) for start in flags["columns"]]

    def rest_of(value):
        for at in range(3, len(ctx_flips())):
            value = grown(value, ctx_step(at)(value))
        if per_sequence > 1:
            value = jnp.sum(value.astype(F32)[gathered_place(ctx, table)], axis=1)
        return value

    def placed(sources, counts, plan, carried=()):
        width = sum(sources[piece[0]].shape[-1] for piece in plan[0][0])
        outs = [shape_of((count, adapters, rank, width), F32) for count in counts]
        return call(
            functools.partial(place_body, rank, len(sources), len(carried), plan),
            (1,),
            [*sources, *carried],
            [whole(x) for x in (*sources, *carried)],
            [(o, whole(o)) for o in outs],
            scalars=[where],
        )

    def place_broad(x):
        return placed([rest_of(value) for value in x], (1, 2), ((((0, 0), (1, 0)),), (((0, 1), (1, 1)), ((0, 2), (1, 2)))))

    sends = [(send, piece.astype(BF)) for send, piece in zip((chip, core, across), cuts[1:])]
    (keep, send), [*got, got_early] = side_by_side(
        lambda x: qkv_back(x, lows, qkv_held, qkv_downs, chunks), grads, sends + [(step1, early)]
    )
    early = grown(early, got_early)
    late = jnp.concatenate(
        [
            cuts[0] + sum(piece.astype(F32) for piece in got),
            up_late.reshape(3 * rank, -1),
            sum(g[1] for g in out_grads),
        ]
    ).astype(BF)[None]
    _, [near_sum, got, got_early] = side_by_side(None, None, [(core, send), (step0, late), (step2, early)])
    early = grown(early, got_early)
    late = jnp.split(grown(late, got), 2, axis=2)
    far = shape_of(grad_resid[0].shape, BF)
    fars = call(
        far_two_body, (1,), [keep, near_sum], [whole(keep), whole(near_sum)], [(far, whole(far))] * chunks
    )
    _, [got0, got_a, got] = side_by_side(
        None, None, [(chip, fars[0]), (step1, late[0]), (step2, broad[1])]
    )
    broad[1] = grown(broad[1], got)
    late[0] = grown(late[0], got_a)
    (grad_down, grad_hidden), [got1, got_a, got_b] = side_by_side(
        place_broad, broad, [(chip, fars[1]), (step2, late[0]), (step1, late[1])]
    )
    late = [grown(late[0], got_a), grown(late[1], got_b)]
    def place_late(x):
        return placed(
            x,
            (6, 5),
            (
                (*[((1, at), (2, at)) for at in (0, 1, 2, 7)], ((0, 1),), ((0, 2),)),
                (*[((1, at), (2, at)) for at in (4, 5, 6, 3)], ((0, 0),)),
            ),
            windows.carried,
        )

    sends, [got_late] = side_by_side(
        lambda x: input_rows(keep, near_sum, x, grad_resid, flags["turn"][0]), [got0, got1], [(step2, late[1])]
    )
    sources = [rest_of(early), rest_of(late[0]), rest_of(grown(late[1], got_late))]
    (grad_wide, grad_model), got = side_by_side(
        place_late, sources, [(return_row(p), rows_back) for p, rows_back in enumerate(sends)]
    )
    input_grad = return_order(got).astype(F32)
    return (output, input_grad, grad_wide, grad_down[0], grad_model, grad_hidden)


def solution(mesh):
    return jax.shard_map(
        on_device,
        mesh=mesh,
        in_specs=(
            P("shard", "ctx", None),
            P("shard", "ctx", None),
            P("shard", None),
            P(None, "shard", None),
            P(None, "shard", None),
            P("shard", None),
            P(None, "shard"),
            P(None, None, None, "shard"),
            P(None, None, "shard"),
            P(None, None, None, "shard"),
            P(None, None, None, "shard"),
        ),
        out_specs=(
            P("shard", "ctx", None),
            P("shard", "ctx", None),
            P(None, None, None, "shard"),
            P(None, None, "shard"),
            P(None, None, None, "shard"),
            P(None, None, None, "shard"),
        ),
        check_vma=False,
    )
```

profile of v0, /device:TPU:0, one launch (start us, length us, event | category | flops | bytes accessed | tf_op | source)
XLA Modules:
  0.0 389.7 jit_solution(10059604539669558550)
XLA Ops:
  12.7 7.1 %collective-permute-start.6 = (bf16[64,2048]{1,0:T(8,128)(2,1)S(1)}, bf16[64,2048]{1,0:T(8,128)(2,1)S(1)}, u32[]{:S(2)}, u32[]{:S(2)}) collective-permute-start(bf16[64,2048]{1,0:T(8,128)(2,1)S(1)} %get-tuple-element.741), channel_id=1, source_target_pairs={{0,12},{1,28},{2,8},{3,24},{4,13},{5,29},{6,9},{7,25},{8,14},{9,30... | collective-permute-start | bytes 786440 | tf_op jit(solution)/shard_map/ppermute | solution.py:1134
  30.8 9.7 %collective-permute-done.4.refs_6_ = bf16[3,128,512]{2,1,0:T(8,128)(2,1)} collective-permute-done((bf16[3,128,512]{2,1,0:T(8,128)(2,1)S(1)}, bf16[3,128,512]{2,1,0:T(8,128)(2,1)}, u32[]{:S(2)}, u32[]{:S(2)}) %collective-permute-start.4) | collective-permute-done | bytes 393248 | tf_op jit(solution)/shard_map/ppermute | solution.py:38
  55.1 7.4 %collective-permute-done.11.refs_10_ = bf16[3,128,512]{2,1,0:T(8,128)(2,1)S(1)} collective-permute-done((bf16[3,128,512]{2,1,0:T(8,128)(2,1)}, bf16[3,128,512]{2,1,0:T(8,128)(2,1)S(1)}, u32[]{:S(2)}, u32[]{:S(2)}) %collective-permute-start.11) | collective-permute-done | bytes 393248 | tf_op jit(solution)/shard_map/ppermute | solution.py:56
  67.6 8.2 %collective-permute-done.13.refs_11_ = bf16[3,128,512]{2,1,0:T(8,128)(2,1)S(1)} collective-permute-done((bf16[3,128,512]{2,1,0:T(8,128)(2,1)S(1)}, bf16[3,128,512]{2,1,0:T(8,128)(2,1)S(1)}, u32[]{:S(2)}, u32[]{:S(2)}) %collective-permute-start.13) | collective-permute-done | bytes 393248 | tf_op jit(solution)/shard_map/ppermute | solution.py:56
  82.7 11.9 %shard_map.167 = (bf16[3,512,512]{2,1,0:T(8,128)(2,1)S(1)}, bf16[3,512,16]{2,1,0:T(8,128)(2,1)S(1)}, f32[24,512]{1,0:T(8,128)S(1)}, bf16[3,2048,512]{2,1,0:T(8,128)(2,1)}) custom-call(s32[2]{0:T(128)S(1)} %pad_add_fusion.places, bf16[160,2048]{1,0:T(8,128)(2,1)S(1)} %get-tuple-element.772.refs_0_.refs_13_, ...), custom_call_target="tpu_custom_call" | custom-call | flops 3221225472 | tf_op jit(solution)/shard_map/pallas_call | solution.py:70
  102.4 6.2 %shard_map.168 = (bf16[512,512]{1,0:T(8,128)(2,1)S(1)}, bf16[512,512]{1,0:T(8,128)(2,1)S(1)}, bf16[512,512]{1,0:T(8,128)(2,1)S(1)}, f32[32,512]{1,0:T(8,128)S(1)}) custom-call(bf16[3,512,512]{2,1,0:T(8,128)(2,1)S(1)} %get-tuple-element.805.refs_0_.refs_1_.refs_2_.refs_3_.refs_4_, ...), custom_call_target="tpu_custom_call" | custom-call | flops 536870912 | tf_op jit(solution)/shard_map/pallas_call | solution.py:70
  121.4 8.0 %collective-permute-done.27.refs_3_ = bf16[1,128,2048]{2,1,0:T(8,128)(2,1)S(1)} collective-permute-done((bf16[1,128,2048]{2,1,0:T(8,128)(2,1)S(1)}, bf16[1,128,2048]{2,1,0:T(8,128)(2,1)S(1)}, u32[]{:S(2)}, u32[]{:S(2)}) %collective-permute-start.27) | collective-permute-done | bytes 524320 | tf_op jit(solution)/shard_map/ppermute | solution.py:38
  153.4 5.0 %collective-permute-done.36.refs_1_ = bf16[64,2048]{1,0:T(8,128)(2,1)S(1)} collective-permute-done((bf16[64,2048]{1,0:T(8,128)(2,1)S(1)}, bf16[64,2048]{1,0:T(8,128)(2,1)S(1)}, u32[]{:S(2)}, u32[]{:S(2)}) %collective-permute-start.36) | collective-permute-done | bytes 262176 | tf_op jit(solution)/shard_map/ppermute | solution.py:38
  167.4 6.5 %collective-permute-done.41.refs_1_ = bf16[64,2048]{1,0:T(8,128)(2,1)S(1)} collective-permute-done((bf16[64,2048]{1,0:T(8,128)(2,1)S(1)}, bf16[64,2048]{1,0:T(8,128)(2,1)S(1)}, u32[]{:S(2)}, u32[]{:S(2)}) %collective-permute-start.41) | collective-permute-done | bytes 262176 | tf_op jit(solution)/shard_map/ppermute | solution.py:38
  177.3 5.9 %shard_map.178 = (bf16[256,2048]{1,0:T(8,128)(2,1)S(1)}, bf16[256,2048]{1,0:T(8,128)(2,1)S(1)}, bf16[256,2048]{1,0:T(8,128)(2,1)S(1)}, bf16[256,32]{1,0:T(8,128)(2,1)S(1)}) custom-call(bf16[64,2048]{1,0:T(8,128)(2,1)S(1)} %get-tuple-element.926.refs_0_, bf16[64,2048]{1,0:T(8,128)(2,1)S(1)} %collective-permute-done.36.refs_1_, ...), custom_call_target="tpu_custom_call" | custom-call | flops 4294967296 | tf_op jit(solution)/shard_map/pallas_call | solution.py:70
  194.3 4.9 %collective-permute-start.49 = (bf16[64,2048]{1,0:T(8,128)(2,1)S(1)}, bf16[64,2048]{1,0:T(8,128)(2,1)S(1)}, u32[]{:S(2)}, u32[]{:S(2)}) collective-permute-start(bf16[64,2048]{1,0:T(8,128)(2,1)S(1)} %get-tuple-element.981), channel_id=1, source_target_pairs={{0,12},{1,28},{2,8},{3,24},{4,13},{5,29},{6,9},{7,25},{8,14},{9,30... | collective-permute-start | bytes 786440 | tf_op jit(solution)/shard_map/ppermute | solution.py:1134
  199.3 5.9 %shard_map.181 = (bf16[256,2048]{1,0:T(8,128)(2,1)S(1)}, bf16[256,2048]{1,0:T(8,128)(2,1)S(1)}, bf16[256,2048]{1,0:T(8,128)(2,1)S(1)}, bf16[256,32]{1,0:T(8,128)(2,1)S(1)}) custom-call(bf16[64,2048]{1,0:T(8,128)(2,1)S(1)} %get-tuple-element.972.refs_0_, bf16[64,2048]{1,0:T(8,128)(2,1)S(1)} %collective-permute-done.41.refs_1_, ...), custom_call_target="tpu_custom_call" | custom-call | flops 4294967296 | tf_op jit(solution)/shard_map/pallas_call | solution.py:70
  220.3 5.1 %shard_map.185 = (bf16[256,2048]{1,0:T(8,128)(2,1)S(1)}, bf16[256,2048]{1,0:T(8,128)(2,1)S(1)}, bf16[256,32]{1,0:T(8,128)(2,1)S(1)}, f32[16,2048]{1,0:T(8,128)S(...) custom-call(bf16[64,2048]{1,0:T(8,128)(2,1)S(1)} %get-tuple-element.1026.refs_0_, ...), custom_call_target="tpu_custom_call" | custom-call | flops 2147483648 | tf_op jit(solution)/shard_map/pallas_call | solution.py:70
  228.5 10.4 %collective-permute-start.57 = (bf16[64,2048]{1,0:T(8,128)(2,1)S(1)}, bf16[64,2048]{1,0:T(8,128)(2,1)S(1)}, u32[]{:S(2)}, u32[]{:S(2)}) collective-permute-start(bf16[64,2048]{1,0:T(8,128)(2,1)S(1)} %get-tuple-element.1065), channel_id=1, source_target_pairs={{0,0},{16,1},{4,2},{20,3},{1,4},{17,5},{5,6},{21,7},{2,8},{18,9},{... | collective-permute-start | bytes 786440 | tf_op jit(solution)/shard_map/ppermute | solution.py:1143
  238.9 5.3 %shard_map.187 = (bf16[128,2048]{1,0:T(8,128)(2,1)S(1)}, bf16[128,2048]{1,0:T(8,128)(2,1)S(1)}, f32[32,2048]{1,0:T(8,128)S(1)}) custom-call(bf16[256,2048]{1,0:T(8,128)(2,1)S(1)} %get-tuple-element.1057.gate_grad, bf16[256,2048]{1,0:T(8,128)(2,1)S(1)} %get-tuple-element.1058.upper_grad, ...), custom_call_target="tpu_custom_call" | custom-call | flops 4294967296 | tf_op jit(solution)/shard_map/pallas_call | solution.py:70
  255.5 5.2 %shard_map.189 = (bf16[256,2048]{1,0:T(8,128)(2,1)S(1)}, bf16[256,2048]{1,0:T(8,128)(2,1)S(1)}, bf16[256,32]{1,0:T(8,128)(2,1)S(1)}, f32[16,2048]{1,0:T(8,128)S(...) custom-call(bf16[64,2048]{1,0:T(8,128)(2,1)S(1)} %get-tuple-element.1091.refs_0_, ...), custom_call_target="tpu_custom_call" | custom-call | flops 2147483648 | tf_op jit(solution)/shard_map/pallas_call | solution.py:70
  260.7 8.4 %collective-permute-done.61 = bf16[64,2048]{1,0:T(8,128)(2,1)S(1)} collective-permute-done((bf16[64,2048]{1,0:T(8,128)(2,1)S(1)}, bf16[64,2048]{1,0:T(8,128)(2,1)S(1)}, u32[]{:S(2)}, u32[]{:S(2)}) %collective-permute-start.61) | collective-permute-done | bytes 262176 | tf_op jit(solution)/shard_map/ppermute | solution.py:1143
  271.9 5.3 %shard_map.191 = (bf16[128,2048]{1,0:T(8,128)(2,1)S(1)}, bf16[128,2048]{1,0:T(8,128)(2,1)S(1)}, f32[32,2048]{1,0:T(8,128)S(1)}) custom-call(bf16[256,2048]{1,0:T(8,128)(2,1)S(1)} %get-tuple-element.1131.gate_grad, bf16[256,2048]{1,0:T(8,128)(2,1)S(1)} %get-tuple-element.1132.upper_grad, ...), custom_call_target="tpu_custom_call" | custom-call | flops 4294967296 | tf_op jit(solution)/shard_map/pallas_call | solution.py:70
  284.5 5.3 %collective-permute-done.70 = bf16[48,512]{1,0:T(8,128)(2,1)S(1)} collective-permute-done((bf16[48,512]{1,0:T(8,128)(2,1)S(1)}, bf16[48,512]{1,0:T(8,128)(2,1)S(1)}, u32[]{:S(2)}, u32[]{:S(2)}) %collective-permute-start.70) | collective-permute-done | bytes 49184 | tf_op jit(solution)/shard_map/ppermute | solution.py:38
  309.6 7.5 %shard_map.196 = (bf16[512,512]{1,0:T(8,128)(2,1)S(1)}, bf16[512,512]{1,0:T(8,128)(2,1)S(1)}, bf16[512,512]{1,0:T(8,128)(2,1)S(1)}, f32[16,512]{1,0:T(8,128)S(1)}) custom-call(bf16[512,512]{1,0:T(8,128)(2,1)S(1)} %copy-done.33, bf16[512,512]{1,0:T(8,128)(2,1)S(1)} %copy-done.35, ...), custom_call_target="tpu_custom_call" | custom-call | flops 1342177280 | tf_op jit(solution)/shard_map/pallas_call | solution.py:70
  346.5 5.9 %collective-permute-done.89 = bf16[2,128,256]{2,1,0:T(8,128)(2,1)S(1)} collective-permute-done((bf16[2,128,256]{2,1,0:T(8,128)(2,1)S(1)}, bf16[2,128,256]{2,1,0:T(8,128)(2,1)S(1)}, u32[]{:S(2)}, u32[]{:S(2)}) %collective-permute-start.89) | collective-permute-done | bytes 131104 | tf_op jit(solution)/shard_map/ppermute | solution.py:56
  362.5 4.9 %collective-permute-done.94 = bf16[4,128,256]{2,1,0:T(8,128)(2,1)S(1)} collective-permute-done((bf16[4,128,256]{2,1,0:T(8,128)(2,1)S(1)}, bf16[4,128,256]{2,1,0:T(8,128)(2,1)S(1)}, u32[]{:S(2)}, u32[]{:S(2)}) %collective-permute-start.94) | collective-permute-done | bytes 262176 | tf_op jit(solution)/shard_map/ppermute | solution.py:56
  368.2 5.4 %collective-permute-start.96 = (bf16[64,2048]{1,0:T(8,128)(2,1)S(1)}, bf16[64,2048]{1,0:T(8,128)(2,1)S(1)}, u32[]{:S(2)}, u32[]{:S(2)}) collective-permute-start(bf16[64,2048]{1,0:T(8,128)(2,1)S(1)} %get-tuple-element.1371), channel_id=1, source_target_pairs={{12,0},{28,1},{8,2},{24,3},{13,4},{29,5},{9,6},{25,7},{14,8},{30,9... | collective-permute-start | bytes 786440 | tf_op jit(solution)/shard_map/ppermute | solution.py:1143
  375.8 11.7 %collective-permute-done.96 = bf16[64,2048]{1,0:T(8,128)(2,1)S(1)} collective-permute-done((bf16[64,2048]{1,0:T(8,128)(2,1)S(1)}, bf16[64,2048]{1,0:T(8,128)(2,1)S(1)}, u32[]{:S(2)}, u32[]{:S(2)}) %collective-permute-start.96) | collective-permute-done | bytes 262176 | tf_op jit(solution)/shard_map/ppermute | solution.py:1143
  (498 shorter events, 219.8 us)
Async XLA Ops:
  9.7 30.9 %collective-permute-start.7 = (bf16[3,512,512]{2,1,0:T(8,128)(2,1)S(1)}, bf16[3,512,512]{2,1,0:T(8,128)(2,1)}, u32[]{:S(2)}, u32[]{:S(2)}) collective-permute-start(bf16[3,512,512]{2,1,0:T(8,128)(2,1)S(1)} %get-tuple-element.742), channel_id=1, source_target_pairs={{0,1},{1,0},{2,3},{3,2},{4,5},{5,4},{6,7},{7,6},{8,9},{9,8},{10,11... | collective-permute-start | bytes 4718600 | tf_op jit(solution)/shard_map/ppermute | solution.py:38
  10.1 20.7 %collective-permute-start.3 = (bf16[3,128,512]{2,1,0:T(8,128)(2,1)S(1)}, bf16[3,128,512]{2,1,0:T(8,128)(2,1)}, u32[]{:S(2)}, u32[]{:S(2)}) collective-permute-start(bf16[3,128,512]{2,1,0:T(8,128)(2,1)S(1)} %get-tuple-element.738), channel_id=1, source_target_pairs={{0,2},{1,3},{2,0},{3,1},{4,6},{5,7},{6,4},{7,5},{8,10},{9,11},{10,... | collective-permute-start | bytes 1179656 | tf_op jit(solution)/shard_map/ppermute | solution.py:38
  11.9 28.7 %collective-permute-start.4 = (bf16[3,128,512]{2,1,0:T(8,128)(2,1)S(1)}, bf16[3,128,512]{2,1,0:T(8,128)(2,1)}, u32[]{:S(2)}, u32[]{:S(2)}) collective-permute-start(bf16[3,128,512]{2,1,0:T(8,128)(2,1)S(1)} %get-tuple-element.739), channel_id=1, source_target_pairs={{0,3},{1,2},{2,1},{3,0},{4,7},{5,6},{6,5},{7,4},{8,11},{9,10},{10,... | collective-permute-start | bytes 1179656 | tf_op jit(solution)/shard_map/ppermute | solution.py:38
  12.0 16.1 %collective-permute-start.5 = (bf16[64,2048]{1,0:T(8,128)(2,1)S(1)}, bf16[64,2048]{1,0:T(8,128)(2,1)S(1)}, u32[]{:S(2)}, u32[]{:S(2)}) collective-permute-start(bf16[64,2048]{1,0:T(8,128)(2,1)S(1)} %get-tuple-element.740), channel_id=1, source_target_pairs={{0,0},{1,16},{2,4},{3,20},{4,1},{5,17},{6,5},{7,21},{8,2},{9,18},{... | collective-permute-start | bytes 786440 | tf_op jit(solution)/shard_map/ppermute | solution.py:1134
  12.7 18.1 %collective-permute-start.6 = (bf16[64,2048]{1,0:T(8,128)(2,1)S(1)}, bf16[64,2048]{1,0:T(8,128)(2,1)S(1)}, u32[]{:S(2)}, u32[]{:S(2)}) collective-permute-start(bf16[64,2048]{1,0:T(8,128)(2,1)S(1)} %get-tuple-element.741), channel_id=1, source_target_pairs={{0,12},{1,28},{2,8},{3,24},{4,13},{5,29},{6,9},{7,25},{8,14},{9,30... | collective-permute-start | bytes 786440 | tf_op jit(solution)/shard_map/ppermute | solution.py:1134
  40.7 23.3 %collective-permute-start.12 = (bf16[160,2048]{1,0:T(8,128)(2,1)S(1)}, bf16[160,2048]{1,0:T(8,128)(2,1)S(1)}, u32[]{:S(2)}, u32[]{:S(2)}) collective-permute-start(bf16[160,2048]{1,0:T(8,128)(2,1)S(1)} %get-tuple-element.772.refs_0_.refs_13_), channel_id=1, source_target_pairs={{0,2},{1,3},{2,0},{3,1},{4,6},{5,7},{6,4},{7,5},{8,10},{9,11},{10,... | collective-permute-start | bytes 1966088 | tf_op jit(solution)/shard_map/ppermute | solution.py:38
  43.1 19.5 %collective-permute-start.11 = (bf16[3,128,512]{2,1,0:T(8,128)(2,1)}, bf16[3,128,512]{2,1,0:T(8,128)(2,1)S(1)}, u32[]{:S(2)}, u32[]{:S(2)}) collective-permute-start(bf16[3,128,512]{2,1,0:T(8,128)(2,1)} %collective-permute-done.4.refs_6_), channel_id=1, source_target_pairs={{0,8},{4,12},{8,0},{12,4},{16,24},{20,28},{24,16},{28,20},{1,9},{5... | collective-permute-start | bytes 1179656 | tf_op jit(solution)/shard_map/ppermute | solution.py:56
  44.9 17.6 %collective-permute-start.8 = (bf16[3,128,512]{2,1,0:T(8,128)(2,1)}, bf16[3,128,512]{2,1,0:T(8,128)(2,1)S(1)}, u32[]{:S(2)}, u32[]{:S(2)}) collective-permute-start(bf16[3,128,512]{2,1,0:T(8,128)(2,1)} %collective-permute-done.3.refs_5_), channel_id=1, source_target_pairs={{0,4},{4,0},{8,12},{12,8},{16,20},{20,16},{24,28},{28,24},{1,5},{5... | collective-permute-start | bytes 1179656 | tf_op jit(solution)/shard_map/ppermute | solution.py:56
  45.0 19.1 %collective-permute-start.9 = (bf16[3,128,512]{2,1,0:T(8,128)(2,1)}, bf16[3,128,512]{2,1,0:T(8,128)(2,1)S(1)}, u32[]{:S(2)}, u32[]{:S(2)}) collective-permute-start(bf16[3,128,512]{2,1,0:T(8,128)(2,1)} %collective-permute-done.4.refs_6_), channel_id=1, source_target_pairs={{0,4},{4,0},{8,12},{12,8},{16,20},{20,16},{24,28},{28,24},{1,5},{5... | collective-permute-start | bytes 1179656 | tf_op jit(solution)/shard_map/ppermute | solution.py:56
  64.1 14.4 %collective-permute-start.15 = (bf16[2,160,2048]{2,1,0:T(8,128)(2,1)S(1)}, bf16[2,160,2048]{2,1,0:T(8,128)(2,1)S(1)}, u32[]{:S(2)}, u32[]{:S(2)}) collective-permute-start(bf16[2,160,2048]{2,1,0:T(8,128)(2,1)S(1)} %pad_maximum_fusion), channel_id=1, source_target_pairs={{0,1},{1,0},{2,3},{3,2},{4,5},{5,4},{6,7},{7,6},{8,9},{9,8},{10,11... | collective-permute-start | bytes 3932168 | tf_op jit(solution)/shard_map/ppermute | solution.py:38
  64.2 14.3 %collective-permute-start.16 = (bf16[1,128,2048]{2,1,0:T(8,128)(2,1)S(1)}, bf16[1,128,2048]{2,1,0:T(8,128)(2,1)S(1)}, u32[]{:S(2)}, u32[]{:S(2)}) collective-permute-start(bf16[1,128,2048]{2,1,0:T(8,128)(2,1)S(1)} %get-tuple-element.765), channel_id=1, source_target_pairs={{0,2},{1,3},{2,0},{3,1},{4,6},{5,7},{6,4},{7,5},{8,10},{9,11},{10,... | collective-permute-start | bytes 1572872 | tf_op jit(solution)/shard_map/ppermute | solution.py:38
  78.6 16.8 %collective-permute-start.20 = (bf16[2,512,2048]{2,1,0:T(8,128)(2,1)S(1)}, bf16[2,512,2048]{2,1,0:T(8,128)(2,1)S(1)}, u32[]{:S(2)}, u32[]{:S(2)}) collective-permute-start(bf16[2,512,2048]{2,1,0:T(8,128)(2,1)S(1)} %get-tuple-element.788), channel_id=1, source_target_pairs={{0,1},{1,0},{2,3},{3,2},{4,5},{5,4},{6,7},{7,6},{8,9},{9,8},{10,11... | collective-permute-start | bytes 12582920 | tf_op jit(solution)/shard_map/ppermute | solution.py:38
  78.7 16.7 %collective-permute-start.17 = (bf16[1,128,2048]{2,1,0:T(8,128)(2,1)S(1)}, bf16[1,128,2048]{2,1,0:T(8,128)(2,1)S(1)}, u32[]{:S(2)}, u32[]{:S(2)}) collective-permute-start(bf16[1,128,2048]{2,1,0:T(8,128)(2,1)S(1)} %get-tuple-element.785), channel_id=1, source_target_pairs={{0,3},{1,2},{2,1},{3,0},{4,7},{5,6},{6,5},{7,4},{8,11},{9,10},{10,... | collective-permute-start | bytes 1572872 | tf_op jit(solution)/shard_map/ppermute | solution.py:38
  79.2 16.2 %collective-permute-start.18 = (bf16[1,128,2048]{2,1,0:T(8,128)(2,1)S(1)}, bf16[1,128,2048]{2,1,0:T(8,128)(2,1)S(1)}, u32[]{:S(2)}, u32[]{:S(2)}) collective-permute-start(bf16[1,128,2048]{2,1,0:T(8,128)(2,1)S(1)} %collective-permute-done.16.refs_2_), channel_id=1, source_target_pairs={{0,4},{4,0},{8,12},{12,8},{16,20},{20,16},{24,28},{28,24},{1,5},{5... | collective-permute-start | bytes 1572872 | tf_op jit(solution)/shard_map/ppermute | solution.py:56
  80.8 14.6 %collective-permute-start.19 = (bf16[1,128,2048]{2,1,0:T(8,128)(2,1)S(1)}, bf16[1,128,2048]{2,1,0:T(8,128)(2,1)S(1)}, u32[]{:S(2)}, u32[]{:S(2)}) collective-permute-start(bf16[1,128,2048]{2,1,0:T(8,128)(2,1)S(1)} %collective-permute-done.16.refs_2_), channel_id=1, source_target_pairs={{0,8},{4,12},{8,0},{12,4},{16,24},{20,28},{24,16},{28,20},{1,9},{5... | collective-permute-start | bytes 1572872 | tf_op jit(solution)/shard_map/ppermute | solution.py:56
  99.8 14.3 %collective-permute-start.24 = (bf16[1,128,2048]{2,1,0:T(8,128)(2,1)S(1)}, bf16[1,128,2048]{2,1,0:T(8,128)(2,1)S(1)}, u32[]{:S(2)}, u32[]{:S(2)}) collective-permute-start(bf16[1,128,2048]{2,1,0:T(8,128)(2,1)S(1)} %get-tuple-element.816), channel_id=1, source_target_pairs={{0,2},{1,3},{2,0},{3,1},{4,6},{5,7},{6,4},{7,5},{8,10},{9,11},{10,... | collective-permute-start | bytes 1572872 | tf_op jit(solution)/shard_map/ppermute | solution.py:38
  115.4 14.5 %collective-permute-start.28 = (bf16[1,128,2048]{2,1,0:T(8,128)(2,1)S(1)}, bf16[1,128,2048]{2,1,0:T(8,128)(2,1)S(1)}, u32[]{:S(2)}, u32[]{:S(2)}) collective-permute-start(bf16[1,128,2048]{2,1,0:T(8,128)(2,1)S(1)} %collective-permute-done.24.refs_2_), channel_id=1, source_target_pairs={{0,4},{4,0},{8,12},{12,8},{16,20},{20,16},{24,28},{28,24},{1,5},{5... | collective-permute-start | bytes 1572872 | tf_op jit(solution)/shard_map/ppermute | solution.py:56
  116.7 14.6 %collective-permute-start.29 = (bf16[1,128,2048]{2,1,0:T(8,128)(2,1)S(1)}, bf16[1,128,2048]{2,1,0:T(8,128)(2,1)S(1)}, u32[]{:S(2)}, u32[]{:S(2)}) collective-permute-start(bf16[1,128,2048]{2,1,0:T(8,128)(2,1)S(1)} %collective-permute-done.24.refs_2_), channel_id=1, source_target_pairs={{0,8},{4,12},{8,0},{12,4},{16,24},{20,28},{24,16},{28,20},{1,9},{5... | collective-permute-start | bytes 1572872 | tf_op jit(solution)/shard_map/ppermute | solution.py:56
  134.0 15.0 %collective-permute-start.34 = (bf16[1,128,2048]{2,1,0:T(8,128)(2,1)S(1)}, bf16[1,128,2048]{2,1,0:T(8,128)(2,1)S(1)}, u32[]{:S(2)}, u32[]{:S(2)}) collective-permute-start(bf16[1,128,2048]{2,1,0:T(8,128)(2,1)S(1)} %collective-permute-done.19.refs_6_), channel_id=1, source_target_pairs={{0,4},{4,0},{8,12},{12,8},{16,20},{20,16},{24,28},{28,24},{1,5},{5... | collective-permute-start | bytes 1572872 | tf_op jit(solution)/shard_map/ppermute | solution.py:56
  227.5 16.7 %collective-permute-start.55 = (bf16[64,2048]{1,0:T(8,128)(2,1)S(1)}, bf16[64,2048]{1,0:T(8,128)(2,1)S(1)}, u32[]{:S(2)}, u32[]{:S(2)}) collective-permute-start(bf16[64,2048]{1,0:T(8,128)(2,1)S(1)} %get-tuple-element.1091.refs_0_), channel_id=1, source_target_pairs={{0,2},{1,3},{2,0},{3,1},{4,6},{5,7},{6,4},{7,5},{8,10},{9,11},{10,... | collective-permute-start | bytes 786440 | tf_op jit(solution)/shard_map/ppermute | solution.py:38
  228.5 15.8 %collective-permute-start.56 = (bf16[64,2048]{1,0:T(8,128)(2,1)S(1)}, bf16[64,2048]{1,0:T(8,128)(2,1)S(1)}, u32[]{:S(2)}, u32[]{:S(2)}) collective-permute-start(bf16[64,2048]{1,0:T(8,128)(2,1)S(1)} %get-tuple-element.1091.refs_0_), channel_id=1, source_target_pairs={{0,1},{1,0},{2,3},{3,2},{4,5},{5,4},{6,7},{7,6},{8,9},{9,8},{10,11... | collective-permute-start | bytes 786440 | tf_op jit(solution)/shard_map/ppermute | solution.py:38
  228.5 15.8 %collective-permute-start.57 = (bf16[64,2048]{1,0:T(8,128)(2,1)S(1)}, bf16[64,2048]{1,0:T(8,128)(2,1)S(1)}, u32[]{:S(2)}, u32[]{:S(2)}) collective-permute-start(bf16[64,2048]{1,0:T(8,128)(2,1)S(1)} %get-tuple-element.1065), channel_id=1, source_target_pairs={{0,0},{16,1},{4,2},{20,3},{1,4},{17,5},{5,6},{21,7},{2,8},{18,9},{... | collective-permute-start | bytes 786440 | tf_op jit(solution)/shard_map/ppermute | solution.py:1143
  252.1 17.1 %collective-permute-start.61 = (bf16[64,2048]{1,0:T(8,128)(2,1)S(1)}, bf16[64,2048]{1,0:T(8,128)(2,1)S(1)}, u32[]{:S(2)}, u32[]{:S(2)}) collective-permute-start(bf16[64,2048]{1,0:T(8,128)(2,1)S(1)} %get-tuple-element.1106), channel_id=1, source_target_pairs={{12,0},{28,1},{8,2},{24,3},{13,4},{29,5},{9,6},{25,7},{14,8},{30,9... | collective-permute-start | bytes 786440 | tf_op jit(solution)/shard_map/ppermute | solution.py:1143
  368.2 19.4 %collective-permute-start.96 = (bf16[64,2048]{1,0:T(8,128)(2,1)S(1)}, bf16[64,2048]{1,0:T(8,128)(2,1)S(1)}, u32[]{:S(2)}, u32[]{:S(2)}) collective-permute-start(bf16[64,2048]{1,0:T(8,128)(2,1)S(1)} %get-tuple-element.1371), channel_id=1, source_target_pairs={{12,0},{28,1},{8,2},{24,3},{13,4},{29,5},{9,6},{25,7},{14,8},{30,9... | collective-permute-start | bytes 786440 | tf_op jit(solution)/shard_map/ppermute | solution.py:1143
  (169 other events, 2140.9 us)
where the time goes:
time: 395 us; the launch traced here: 390 us
  waiting for transfers between devices  153 us (39%)
  starting transfers between devices  112 us (28%)
  Pallas kernels  104 us (26%)
  local copies, waits for them, and re-layouts  10.2 us (3%)
  other arithmetic  6.27 us (2%)
    pallas_call x40, Pallas kernels, call(): pl.pallas_call(body, grid_spec=pltpu.PrefetchScalarGridSpec(num_scalar_pr...  104 us
    ppermute x57, waiting for transfers between devices, over_shard(): return lax.ppermute(value, 'shard', [(i, i ^ flip) for i in range(size)])  72.2 us
    ppermute x32, waiting for transfers between devices, over_ctx(): return lax.ppermute(value, 'ctx', [(i, i ^ flip) for i in range(size)])  56.8 us
    ppermute x57, starting transfers between devices, over_shard(): return lax.ppermute(value, 'shard', [(i, i ^ flip) for i in range(size)])  44.8 us
    ppermute x32, starting transfers between devices, over_ctx(): return lax.ppermute(value, 'ctx', [(i, i ^ flip) for i in range(size)])  34.1 us
    ppermute x4, waiting for transfers between devices, return_row(): lax.ppermute(cut, ('ctx', 'shard'), [(b, a) for a, b in pairs[p]])  20.1 us
    ppermute x4, starting transfers between devices, return_row(): lax.ppermute(cut, ('ctx', 'shard'), [(b, a) for a, b in pairs[p]])  19.8 us
    ppermute x4, starting transfers between devices, send_row(): return lambda cut: lax.ppermute(cut, ('ctx', 'shard'), pairs[p])  13.6 us
  transfers between devices with their start and end apart: 97, of which 52 were waited for; matrix products, arithmetic and copies ran while one was open for 1% of the time, Pallas kernels for 24%

commit v1 on v0

--- a/solution.py
+++ b/solution.py
@@ -3,6 +3,7 @@
 
 import jax
 import jax.numpy as jnp
+import numpy as np
 from jax import lax
 from jax.experimental import pallas as pl
 from jax.experimental.pallas import tpu as pltpu
@@ -927,6 +928,21 @@
     )
 
 
+def order_body(spot, *refs):
+    gots, out = refs[:-1], refs[-1]
+    for turn in range(len(gots)):
+
+        @pl.when(spot[0] == turn)
+        def _():
+            for j in range(len(gots)):
+                out[j] = gots[(j - turn) % len(gots)][...].astype(F32)
+
+
+def order_rows(gots, spot):
+    out = shape_of((len(gots), *gots[0].shape), F32)
+    return call(order_body, (1,), gots, [whole(x) for x in gots], [(out, whole(out))], scalars=[spot])[0]
+
+
 def by_rows(body, args, kinds):
     *lead, rows, width = args[0].shape
     outs = [shape_of((*lead, rows // 2, width), kind) for kind in kinds]
@@ -1111,6 +1127,7 @@
         "columns": [((shard ^ flip) * wide).astype(jnp.uint32) for flip in FLIPS],
         "places": jnp.stack([shard, ctx % 4]).astype(jnp.int32),
         "turn": [((my_slot - p) % seqs)[None].astype(jnp.int32) for p in range(seqs)],
+        "spot": my_spot[None].astype(jnp.int32),
     }
 
     def pick(parts, is_it):
@@ -1192,47 +1209,43 @@
     row_cuts = cut_rows(tokens)
 
     def rope_tables(place):
-        shape = (chunks, shards, rows, HD)
-        spot, turn, row, lane = [lax.broadcasted_iota(jnp.int32, shape, axis) for axis in range(4)]
-        owner = place ^ (turn // 2 + turn % 2 * 2)
+        spot, turn, row = np.indices((chunks, shards, rows)).reshape(3, -1).astype(np.int32)
+        owner = place ^ np.array(FLIPS, np.int32)[turn]
         position = my_part * group_rows + (spot * shards + owner) * rows + row
-        freqs = jnp.exp((lane % (HD // 2)).astype(F32) * (-2.0 * math.log(rope_base) / HD))
-        angles = position.astype(F32) * freqs
-        sine = jnp.sin(angles) * jnp.where(lane < HD // 2, -1.0, 1.0)
-        return position[..., 0].reshape(-1), jnp.cos(angles).reshape(-1, HD), sine.reshape(-1, HD)
+        lane = np.arange(HD)
+        freqs = np.exp((lane % (HD // 2)) * (-2.0 * math.log(rope_base) / HD)).astype(np.float32)
+        angles = position.astype(F32)[:, None] * freqs[None, :]
+        sign = np.where(lane < HD // 2, -1.0, 1.0).astype(np.float32)
+        return position, jnp.cos(angles), jnp.sin(angles) * sign
 
     def prepare(x):
         chosen = choose(x[0], a_wide, a_down, b_model, b_hidden, gains)
         return chosen, cut(x[1], 0, 2, x[2], True), x[3], rope_tables(x[2][0])
 
-    (chosen, gate_up_cuts, where, (positions, cosine, sine)), [qkv_a, qkv_b, *row_got, qkv_near] = side_by_side(
+    (chosen, gate_up_cuts, where, (positions, cosine, sine)), [qkv_a, *row_got, qkv_near] = side_by_side(
         prepare,
         [index_all[my_sequence][None], w_gate_up, places, where],
-        [
-            (chip, qkv_far),
-            (across, qkv_cross),
-            (send_row(0), row_cuts[0]),
-            (send_row(1), row_cuts[1]),
-            (core, qkv_near),
-        ],
+        [(chip, qkv_far), (send_row(0), row_cuts[0]), (send_row(1), row_cuts[1]), (core, qkv_near)],
     )
     own_wide, own_down, own_model, own_hidden, small = chosen
     near, gate_far, gate_cross, up_far, up_cross = gate_up_cuts
 
     token_rows = chunk_order(row_got)
-    token_own = jnp.concatenate([*token_rows, small])
     held = {}
 
-    def load_out(weights):
-        held["out"], held["down"], done = load_plain(*weights)
-        return done
-
-    done, [qkv_xa, qkv_xb, qkv_za, qkv_zb, token_far] = side_by_side(
+    def load_out(x):
+        held["out"], held["down"], done = load_plain(*x[:2])
+        return done, jnp.concatenate(x[2:])
+
+    (done, token_own), [qkv_b, qkv_xa, qkv_za] = side_by_side(
         load_out,
-        [w_attn, w_down],
-        [(by_x, qkv_a), (by_x, qkv_b), (by_z, qkv_a), (by_z, qkv_b), (chip, token_own)],
+        [w_attn, w_down, *token_rows, small],
+        [(across, qkv_cross), (by_x, qkv_a), (by_z, qkv_a)],
     )
     windows.carried.append(done)
+    _, [token_far, qkv_xb, qkv_zb] = side_by_side(
+        None, None, [(chip, token_own), (by_x, qkv_b), (by_z, qkv_b)]
+    )
     _, [last_a, last_b, token_near, gate_a] = side_by_side(
         None,
         None,
@@ -1533,7 +1546,7 @@
     (grad_wide, grad_model), got = side_by_side(
         place_late, sources, [(return_row(p), rows_back) for p, rows_back in enumerate(sends)]
     )
-    input_grad = return_order(got).astype(F32)
+    input_grad = order_rows(got, flags["spot"])
     return (output, input_grad, grad_wide, grad_down[0], grad_model, grad_hidden)
 
 

time: 395 us -> 392 us (level)
    ppermute x57, waiting for transfers between devices: 72.2 us -> 66.4 us  [over_shard(): return lax.ppermute(value, 'shard', [(i, i ^ flip) for i in range(size)])]
    pallas_call x40 -> x41, Pallas kernels: 104 us -> 106 us  [call(): pl.pallas_call(body, grid_spec=pltpu.PrefetchScalarGridSpec(num_scalar_pr...]
    unnamed x192 -> x194, local copies, waits for them, and re-layouts: 8.29 us -> 7.47 us
  transfers between devices with their start and end apart: 97 -> 97, of which waited for: 52 -> 53; matrix products, arithmetic and copies ran while one was open for 1% -> 1% of each run, Pallas kernels for 24% -> 24%
where the time goes in v1:
time: 392 us; the launch traced here: 387 us
  waiting for transfers between devices  153 us (39%)
  starting transfers between devices  112 us (29%)
  Pallas kernels  106 us (27%)
  local copies, waits for them, and re-layouts  8.23 us (2%)
  other arithmetic  4.92 us (1%)
    pallas_call x41, Pallas kernels, call(): pl.pallas_call(body, grid_spec=pltpu.PrefetchScalarGridSpec(num_scalar_pr...  106 us
    ppermute x57, waiting for transfers between devices, over_shard(): return lax.ppermute(value, 'shard', [(i, i ^ flip) for i in range(size)])  66.4 us
    ppermute x32, waiting for transfers between devices, over_ctx(): return lax.ppermute(value, 'ctx', [(i, i ^ flip) for i in range(size)])  59.4 us
    ppermute x57, starting transfers between devices, over_shard(): return lax.ppermute(value, 'shard', [(i, i ^ flip) for i in range(size)])  47.9 us
    ppermute x32, starting transfers between devices, over_ctx(): return lax.ppermute(value, 'ctx', [(i, i ^ flip) for i in range(size)])  32.6 us
    ppermute x4, starting transfers between devices, return_row(): lax.ppermute(cut, ('ctx', 'shard'), [(b, a) for a, b in pairs[p]])  19.6 us
    ppermute x4, waiting for transfers between devices, return_row(): lax.ppermute(cut, ('ctx', 'shard'), [(b, a) for a, b in pairs[p]])  19.2 us
    ppermute x4, starting transfers between devices, send_row(): return lambda cut: lax.ppermute(cut, ('ctx', 'shard'), pairs[p])  12 us
  transfers between devices with their start and end apart: 97, of which 53 were waited for; matrix products, arithmetic and copies ran while one was open for 1% of the time, Pallas kernels for 24%

profile of v1, /device:TPU:0, one launch (start us, length us, event | category | flops | bytes accessed | tf_op | source)
XLA Modules:
  0.0 386.9 jit_solution(2035322366709380458)
XLA Ops:
  12.4 5.7 %collective-permute-start.5 = (bf16[64,2048]{1,0:T(8,128)(2,1)S(1)}, bf16[64,2048]{1,0:T(8,128)(2,1)S(1)}, u32[]{:S(2)}, u32[]{:S(2)}) collective-permute-start(bf16[64,2048]{1,0:T(8,128)(2,1)S(1)} %get-tuple-element.748), channel_id=1, source_target_pairs={{0,12},{1,28},{2,8},{3,24},{4,13},{5,29},{6,9},{7,25},{8,14},{9,30... | collective-permute-start | bytes 786440 | tf_op jit(solution)/shard_map/ppermute | solution.py:1151
  25.2 6.4 %collective-permute-done.5 = bf16[64,2048]{1,0:T(8,128)(2,1)S(1)} collective-permute-done((bf16[64,2048]{1,0:T(8,128)(2,1)S(1)}, bf16[64,2048]{1,0:T(8,128)(2,1)S(1)}, u32[]{:S(2)}, u32[]{:S(2)}) %collective-permute-start.5) | collective-permute-done | bytes 262176 | tf_op jit(solution)/shard_map/ppermute | solution.py:1151
  49.5 7.6 %collective-permute-done.11.refs_8_ = bf16[3,128,512]{2,1,0:T(8,128)(2,1)S(1)} collective-permute-done((bf16[3,128,512]{2,1,0:T(8,128)(2,1)S(1)}, bf16[3,128,512]{2,1,0:T(8,128)(2,1)S(1)}, u32[]{:S(2)}, u32[]{:S(2)}) %collective-permute-start.11) | collective-permute-done | bytes 393248 | tf_op jit(solution)/shard_map/ppermute | solution.py:57
  66.2 8.3 %collective-permute-done.13.refs_11_ = bf16[3,128,512]{2,1,0:T(8,128)(2,1)S(1)} collective-permute-done((bf16[3,128,512]{2,1,0:T(8,128)(2,1)S(1)}, bf16[3,128,512]{2,1,0:T(8,128)(2,1)S(1)}, u32[]{:S(2)}, u32[]{:S(2)}) %collective-permute-start.13) | collective-permute-done | bytes 393248 | tf_op jit(solution)/shard_map/ppermute | solution.py:57
  81.3 11.9 %shard_map.212 = (bf16[3,512,512]{2,1,0:T(8,128)(2,1)S(1)}, bf16[3,512,16]{2,1,0:T(8,128)(2,1)S(1)}, f32[24,512]{1,0:T(8,128)S(1)}, bf16[3,2048,512]{2,1,0:T(8,128)(2,1)}) custom-call(s32[2]{0:T(128)S(1)} %pad_add_fusion.places, bf16[160,2048]{1,0:T(8,128)(2,1)S(1)} %pad_maximum_fusion.3.refs_0_.refs_13_, ...), custom_call_target="tpu_custom_call" | custom-call | flops 3221225472 | tf_op jit(solution)/shard_map/pallas_call | solution.py:71
  100.9 6.2 %shard_map.213 = (bf16[512,512]{1,0:T(8,128)(2,1)S(1)}, bf16[512,512]{1,0:T(8,128)(2,1)S(1)}, bf16[512,512]{1,0:T(8,128)(2,1)S(1)}, f32[32,512]{1,0:T(8,128)S(1)}) custom-call(bf16[3,512,512]{2,1,0:T(8,128)(2,1)S(1)} %get-tuple-element.820.refs_0_.refs_1_.refs_2_.refs_3_.refs_4_, ...), custom_call_target="tpu_custom_call" | custom-call | flops 536870912 | tf_op jit(solution)/shard_map/pallas_call | solution.py:71
  119.4 8.1 %collective-permute-done.27.refs_3_ = bf16[1,128,2048]{2,1,0:T(8,128)(2,1)S(1)} collective-permute-done((bf16[1,128,2048]{2,1,0:T(8,128)(2,1)S(1)}, bf16[1,128,2048]{2,1,0:T(8,128)(2,1)S(1)}, u32[]{:S(2)}, u32[]{:S(2)}) %collective-permute-start.27) | collective-permute-done | bytes 524320 | tf_op jit(solution)/shard_map/ppermute | solution.py:39
  151.6 4.8 %collective-permute-done.36.refs_1_ = bf16[64,2048]{1,0:T(8,128)(2,1)S(1)} collective-permute-done((bf16[64,2048]{1,0:T(8,128)(2,1)S(1)}, bf16[64,2048]{1,0:T(8,128)(2,1)S(1)}, u32[]{:S(2)}, u32[]{:S(2)}) %collective-permute-start.36) | collective-permute-done | bytes 262176 | tf_op jit(solution)/shard_map/ppermute | solution.py:39
  165.6 6.1 %collective-permute-done.41.refs_1_ = bf16[64,2048]{1,0:T(8,128)(2,1)S(1)} collective-permute-done((bf16[64,2048]{1,0:T(8,128)(2,1)S(1)}, bf16[64,2048]{1,0:T(8,128)(2,1)S(1)}, u32[]{:S(2)}, u32[]{:S(2)}) %collective-permute-start.41) | collective-permute-done | bytes 262176 | tf_op jit(solution)/shard_map/ppermute | solution.py:39
  175.6 5.9 %shard_map.223 = (bf16[256,2048]{1,0:T(8,128)(2,1)S(1)}, bf16[256,2048]{1,0:T(8,128)(2,1)S(1)}, bf16[256,2048]{1,0:T(8,128)(2,1)S(1)}, bf16[256,32]{1,0:T(8,128)(2,1)S(1)}) custom-call(bf16[64,2048]{1,0:T(8,128)(2,1)S(1)} %get-tuple-element.941.refs_0_, bf16[64,2048]{1,0:T(8,128)(2,1)S(1)} %collective-permute-done.36.refs_1_, ...), custom_call_target="tpu_custom_call" | custom-call | flops 4294967296 | tf_op jit(solution)/shard_map/pallas_call | solution.py:71
  192.7 4.7 %collective-permute-start.49 = (bf16[64,2048]{1,0:T(8,128)(2,1)S(1)}, bf16[64,2048]{1,0:T(8,128)(2,1)S(1)}, u32[]{:S(2)}, u32[]{:S(2)}) collective-permute-start(bf16[64,2048]{1,0:T(8,128)(2,1)S(1)} %get-tuple-element.996), channel_id=1, source_target_pairs={{0,12},{1,28},{2,8},{3,24},{4,13},{5,29},{6,9},{7,25},{8,14},{9,30... | collective-permute-start | bytes 786440 | tf_op jit(solution)/shard_map/ppermute | solution.py:1151
  197.5 5.9 %shard_map.226 = (bf16[256,2048]{1,0:T(8,128)(2,1)S(1)}, bf16[256,2048]{1,0:T(8,128)(2,1)S(1)}, bf16[256,2048]{1,0:T(8,128)(2,1)S(1)}, bf16[256,32]{1,0:T(8,128)(2,1)S(1)}) custom-call(bf16[64,2048]{1,0:T(8,128)(2,1)S(1)} %get-tuple-element.987.refs_0_, bf16[64,2048]{1,0:T(8,128)(2,1)S(1)} %collective-permute-done.41.refs_1_, ...), custom_call_target="tpu_custom_call" | custom-call | flops 4294967296 | tf_op jit(solution)/shard_map/pallas_call | solution.py:71
  218.1 5.1 %shard_map.230 = (bf16[256,2048]{1,0:T(8,128)(2,1)S(1)}, bf16[256,2048]{1,0:T(8,128)(2,1)S(1)}, bf16[256,32]{1,0:T(8,128)(2,1)S(1)}, f32[16,2048]{1,0:T(8,128)S(...) custom-call(bf16[64,2048]{1,0:T(8,128)(2,1)S(1)} %get-tuple-element.1041.refs_0_, ...), custom_call_target="tpu_custom_call" | custom-call | flops 2147483648 | tf_op jit(solution)/shard_map/pallas_call | solution.py:71
  227.1 10.4 %collective-permute-start.57 = (bf16[64,2048]{1,0:T(8,128)(2,1)S(1)}, bf16[64,2048]{1,0:T(8,128)(2,1)S(1)}, u32[]{:S(2)}, u32[]{:S(2)}) collective-permute-start(bf16[64,2048]{1,0:T(8,128)(2,1)S(1)} %get-tuple-element.1080), channel_id=1, source_target_pairs={{0,0},{16,1},{4,2},{20,3},{1,4},{17,5},{5,6},{21,7},{2,8},{18,9},{... | collective-permute-start | bytes 786440 | tf_op jit(solution)/shard_map/ppermute | solution.py:1160
  237.5 5.3 %shard_map.232 = (bf16[128,2048]{1,0:T(8,128)(2,1)S(1)}, bf16[128,2048]{1,0:T(8,128)(2,1)S(1)}, f32[32,2048]{1,0:T(8,128)S(1)}) custom-call(bf16[256,2048]{1,0:T(8,128)(2,1)S(1)} %get-tuple-element.1072.gate_grad, bf16[256,2048]{1,0:T(8,128)(2,1)S(1)} %get-tuple-element.1073.upper_grad, ...), custom_call_target="tpu_custom_call" | custom-call | flops 4294967296 | tf_op jit(solution)/shard_map/pallas_call | solution.py:71
  253.7 5.2 %shard_map.234 = (bf16[256,2048]{1,0:T(8,128)(2,1)S(1)}, bf16[256,2048]{1,0:T(8,128)(2,1)S(1)}, bf16[256,32]{1,0:T(8,128)(2,1)S(1)}, f32[16,2048]{1,0:T(8,128)S(...) custom-call(bf16[64,2048]{1,0:T(8,128)(2,1)S(1)} %get-tuple-element.1106.refs_0_, ...), custom_call_target="tpu_custom_call" | custom-call | flops 2147483648 | tf_op jit(solution)/shard_map/pallas_call | solution.py:71
  258.9 8.0 %collective-permute-done.61 = bf16[64,2048]{1,0:T(8,128)(2,1)S(1)} collective-permute-done((bf16[64,2048]{1,0:T(8,128)(2,1)S(1)}, bf16[64,2048]{1,0:T(8,128)(2,1)S(1)}, u32[]{:S(2)}, u32[]{:S(2)}) %collective-permute-start.61) | collective-permute-done | bytes 262176 | tf_op jit(solution)/shard_map/ppermute | solution.py:1160
  270.5 5.3 %shard_map.236 = (bf16[128,2048]{1,0:T(8,128)(2,1)S(1)}, bf16[128,2048]{1,0:T(8,128)(2,1)S(1)}, f32[32,2048]{1,0:T(8,128)S(1)}) custom-call(bf16[256,2048]{1,0:T(8,128)(2,1)S(1)} %get-tuple-element.1147.gate_grad, bf16[256,2048]{1,0:T(8,128)(2,1)S(1)} %get-tuple-element.1148.upper_grad, ...), custom_call_target="tpu_custom_call" | custom-call | flops 4294967296 | tf_op jit(solution)/shard_map/pallas_call | solution.py:71
  282.5 5.8 %collective-permute-done.70 = bf16[48,512]{1,0:T(8,128)(2,1)S(1)} collective-permute-done((bf16[48,512]{1,0:T(8,128)(2,1)S(1)}, bf16[48,512]{1,0:T(8,128)(2,1)S(1)}, u32[]{:S(2)}, u32[]{:S(2)}) %collective-permute-start.70) | collective-permute-done | bytes 49184 | tf_op jit(solution)/shard_map/ppermute | solution.py:39
  307.3 7.5 %shard_map.241 = (bf16[512,512]{1,0:T(8,128)(2,1)S(1)}, bf16[512,512]{1,0:T(8,128)(2,1)S(1)}, bf16[512,512]{1,0:T(8,128)(2,1)S(1)}, f32[16,512]{1,0:T(8,128)S(1)}) custom-call(bf16[512,512]{1,0:T(8,128)(2,1)S(1)} %copy-done.32, bf16[512,512]{1,0:T(8,128)(2,1)S(1)} %copy-done.34, ...), custom_call_target="tpu_custom_call" | custom-call | flops 1342177280 | tf_op jit(solution)/shard_map/pallas_call | solution.py:71
  326.7 4.8 %shard_map.243 = (bf16[2,128,2048]{2,1,0:T(8,128)(2,1)S(1)}, bf16[2,128,2048]{2,1,0:T(8,128)(2,1)S(1)}) custom-call(bf16[3,512,512]{2,1,0:T(8,128)(2,1)S(1)} %get-tuple-element.1282.grads, bf16[512,48]{1,0:T(8,128)(2,1)S(1)} %get-tuple-element.1283.lows, bf16[3,2048,512]{2,1,0:T(8,128)(2,1)S(1)} %bitcast.64, bf16[48,2048]{1,0:T(8,128)(2,1)S(1)} %copy-done.30), custom_call_target="tpu_custom_call" | custom-call | flops 3221225472 | tf_op jit(solution)/shard_map/pallas_call | solution.py:71
  344.1 6.1 %collective-permute-done.89 = bf16[2,128,256]{2,1,0:T(8,128)(2,1)S(1)} collective-permute-done((bf16[2,128,256]{2,1,0:T(8,128)(2,1)S(1)}, bf16[2,128,256]{2,1,0:T(8,128)(2,1)S(1)}, u32[]{:S(2)}, u32[]{:S(2)}) %collective-permute-start.89) | collective-permute-done | bytes 131104 | tf_op jit(solution)/shard_map/ppermute | solution.py:57
  366.0 5.2 %collective-permute-start.96 = (bf16[64,2048]{1,0:T(8,128)(2,1)S(1)}, bf16[64,2048]{1,0:T(8,128)(2,1)S(1)}, u32[]{:S(2)}, u32[]{:S(2)}) collective-permute-start(bf16[64,2048]{1,0:T(8,128)(2,1)S(1)} %get-tuple-element.1387), channel_id=1, source_target_pairs={{12,0},{28,1},{8,2},{24,3},{13,4},{29,5},{9,6},{25,7},{14,8},{30,9... | collective-permute-start | bytes 786440 | tf_op jit(solution)/shard_map/ppermute | solution.py:1160
  374.4 11.3 %collective-permute-done.96.refs_1_ = bf16[64,2048]{1,0:T(8,128)(2,1)S(1)} collective-permute-done((bf16[64,2048]{1,0:T(8,128)(2,1)S(1)}, bf16[64,2048]{1,0:T(8,128)(2,1)S(1)}, u32[]{:S(2)}, u32[]{:S(2)}) %collective-permute-start.96) | collective-permute-done | bytes 262176 | tf_op jit(solution)/shard_map/ppermute | solution.py:1160
  (472 shorter events, 222.5 us)
Async XLA Ops:
  9.7 22.3 %collective-permute-start.6 = (bf16[3,512,512]{2,1,0:T(8,128)(2,1)S(1)}, bf16[3,512,512]{2,1,0:T(8,128)(2,1)S(1)}, u32[]{:S(2)}, u32[]{:S(2)}) collective-permute-start(bf16[3,512,512]{2,1,0:T(8,128)(2,1)S(1)} %get-tuple-element.749), channel_id=1, source_target_pairs={{0,1},{1,0},{2,3},{3,2},{4,5},{5,4},{6,7},{7,6},{8,9},{9,8},{10,11... | collective-permute-start | bytes 4718600 | tf_op jit(solution)/shard_map/ppermute | solution.py:39
  10.0 21.9 %collective-permute-start.3 = (bf16[3,128,512]{2,1,0:T(8,128)(2,1)S(1)}, bf16[3,128,512]{2,1,0:T(8,128)(2,1)S(1)}, u32[]{:S(2)}, u32[]{:S(2)}) collective-permute-start(bf16[3,128,512]{2,1,0:T(8,128)(2,1)S(1)} %get-tuple-element.746), channel_id=1, source_target_pairs={{0,2},{1,3},{2,0},{3,1},{4,6},{5,7},{6,4},{7,5},{8,10},{9,11},{10,... | collective-permute-start | bytes 1179656 | tf_op jit(solution)/shard_map/ppermute | solution.py:39
  11.7 13.5 %collective-permute-start.4 = (bf16[64,2048]{1,0:T(8,128)(2,1)S(1)}, bf16[64,2048]{1,0:T(8,128)(2,1)S(1)}, u32[]{:S(2)}, u32[]{:S(2)}) collective-permute-start(bf16[64,2048]{1,0:T(8,128)(2,1)S(1)} %get-tuple-element.747), channel_id=1, source_target_pairs={{0,0},{1,16},{2,4},{3,20},{4,1},{5,17},{6,5},{7,21},{8,2},{9,18},{... | collective-permute-start | bytes 786440 | tf_op jit(solution)/shard_map/ppermute | solution.py:1151
  12.4 19.2 %collective-permute-start.5 = (bf16[64,2048]{1,0:T(8,128)(2,1)S(1)}, bf16[64,2048]{1,0:T(8,128)(2,1)S(1)}, u32[]{:S(2)}, u32[]{:S(2)}) collective-permute-start(bf16[64,2048]{1,0:T(8,128)(2,1)S(1)} %get-tuple-element.748), channel_id=1, source_target_pairs={{0,12},{1,28},{2,8},{3,24},{4,13},{5,29},{6,9},{7,25},{8,14},{9,30... | collective-permute-start | bytes 786440 | tf_op jit(solution)/shard_map/ppermute | solution.py:1151
  45.9 16.5 %collective-permute-start.10 = (bf16[160,2048]{1,0:T(8,128)(2,1)S(1)}, bf16[160,2048]{1,0:T(8,128)(2,1)S(1)}, u32[]{:S(2)}, u32[]{:S(2)}) collective-permute-start(bf16[160,2048]{1,0:T(8,128)(2,1)S(1)} %pad_maximum_fusion.3.refs_0_.refs_13_), channel_id=1, source_target_pairs={{0,2},{1,3},{2,0},{3,1},{4,6},{5,7},{6,4},{7,5},{8,10},{9,11},{10,... | collective-permute-start | bytes 1966088 | tf_op jit(solution)/shard_map/ppermute | solution.py:39
  62.5 14.4 %collective-permute-start.15 = (bf16[2,160,2048]{2,1,0:T(8,128)(2,1)S(1)}, bf16[2,160,2048]{2,1,0:T(8,128)(2,1)S(1)}, u32[]{:S(2)}, u32[]{:S(2)}) collective-permute-start(bf16[2,160,2048]{2,1,0:T(8,128)(2,1)S(1)} %pad_maximum_fusion), channel_id=1, source_target_pairs={{0,1},{1,0},{2,3},{3,2},{4,5},{5,4},{6,7},{7,6},{8,9},{9,8},{10,11... | collective-permute-start | bytes 3932168 | tf_op jit(solution)/shard_map/ppermute | solution.py:39
  62.6 14.3 %collective-permute-start.16 = (bf16[1,128,2048]{2,1,0:T(8,128)(2,1)S(1)}, bf16[1,128,2048]{2,1,0:T(8,128)(2,1)S(1)}, u32[]{:S(2)}, u32[]{:S(2)}) collective-permute-start(bf16[1,128,2048]{2,1,0:T(8,128)(2,1)S(1)} %get-tuple-element.780), channel_id=1, source_target_pairs={{0,2},{1,3},{2,0},{3,1},{4,6},{5,7},{6,4},{7,5},{8,10},{9,11},{10,... | collective-permute-start | bytes 1572872 | tf_op jit(solution)/shard_map/ppermute | solution.py:39
  76.9 17.1 %collective-permute-start.20 = (bf16[2,512,2048]{2,1,0:T(8,128)(2,1)S(1)}, bf16[2,512,2048]{2,1,0:T(8,128)(2,1)S(1)}, u32[]{:S(2)}, u32[]{:S(2)}) collective-permute-start(bf16[2,512,2048]{2,1,0:T(8,128)(2,1)S(1)} %get-tuple-element.803), channel_id=1, source_target_pairs={{0,1},{1,0},{2,3},{3,2},{4,5},{5,4},{6,7},{7,6},{8,9},{9,8},{10,11... | collective-permute-start | bytes 12582920 | tf_op jit(solution)/shard_map/ppermute | solution.py:39
  77.0 17.0 %collective-permute-start.17 = (bf16[1,128,2048]{2,1,0:T(8,128)(2,1)S(1)}, bf16[1,128,2048]{2,1,0:T(8,128)(2,1)S(1)}, u32[]{:S(2)}, u32[]{:S(2)}) collective-permute-start(bf16[1,128,2048]{2,1,0:T(8,128)(2,1)S(1)} %get-tuple-element.800), channel_id=1, source_target_pairs={{0,3},{1,2},{2,1},{3,0},{4,7},{5,6},{6,5},{7,4},{8,11},{9,10},{10,... | collective-permute-start | bytes 1572872 | tf_op jit(solution)/shard_map/ppermute | solution.py:39
  77.9 16.1 %collective-permute-start.18 = (bf16[1,128,2048]{2,1,0:T(8,128)(2,1)S(1)}, bf16[1,128,2048]{2,1,0:T(8,128)(2,1)S(1)}, u32[]{:S(2)}, u32[]{:S(2)}) collective-permute-start(bf16[1,128,2048]{2,1,0:T(8,128)(2,1)S(1)} %collective-permute-done.16.refs_2_), channel_id=1, source_target_pairs={{0,4},{4,0},{8,12},{12,8},{16,20},{20,16},{24,28},{28,24},{1,5},{5... | collective-permute-start | bytes 1572872 | tf_op jit(solution)/shard_map/ppermute | solution.py:57
  79.0 15.0 %collective-permute-start.19 = (bf16[1,128,2048]{2,1,0:T(8,128)(2,1)S(1)}, bf16[1,128,2048]{2,1,0:T(8,128)(2,1)S(1)}, u32[]{:S(2)}, u32[]{:S(2)}) collective-permute-start(bf16[1,128,2048]{2,1,0:T(8,128)(2,1)S(1)} %collective-permute-done.16.refs_2_), channel_id=1, source_target_pairs={{0,8},{4,12},{8,0},{12,4},{16,24},{20,28},{24,16},{28,20},{1,9},{5... | collective-permute-start | bytes 1572872 | tf_op jit(solution)/shard_map/ppermute | solution.py:57
  98.2 14.0 %collective-permute-start.24 = (bf16[1,128,2048]{2,1,0:T(8,128)(2,1)S(1)}, bf16[1,128,2048]{2,1,0:T(8,128)(2,1)S(1)}, u32[]{:S(2)}, u32[]{:S(2)}) collective-permute-start(bf16[1,128,2048]{2,1,0:T(8,128)(2,1)S(1)} %get-tuple-element.831), channel_id=1, source_target_pairs={{0,2},{1,3},{2,0},{3,1},{4,6},{5,7},{6,4},{7,5},{8,10},{9,11},{10,... | collective-permute-start | bytes 1572872 | tf_op jit(solution)/shard_map/ppermute | solution.py:39
  99.5 14.1 %collective-permute-start.25 = (bf16[1,128,2048]{2,1,0:T(8,128)(2,1)S(1)}, bf16[1,128,2048]{2,1,0:T(8,128)(2,1)S(1)}, u32[]{:S(2)}, u32[]{:S(2)}) collective-permute-start(bf16[1,128,2048]{2,1,0:T(8,128)(2,1)S(1)} %collective-permute-done.17.refs_3_), channel_id=1, source_target_pairs={{0,4},{4,0},{8,12},{12,8},{16,20},{20,16},{24,28},{28,24},{1,5},{5... | collective-permute-start | bytes 1572872 | tf_op jit(solution)/shard_map/ppermute | solution.py:57
  100.3 13.8 %collective-permute-start.26 = (bf16[1,128,2048]{2,1,0:T(8,128)(2,1)S(1)}, bf16[1,128,2048]{2,1,0:T(8,128)(2,1)S(1)}, u32[]{:S(2)}, u32[]{:S(2)}) collective-permute-start(bf16[1,128,2048]{2,1,0:T(8,128)(2,1)S(1)} %collective-permute-done.17.refs_3_), channel_id=1, source_target_pairs={{0,8},{4,12},{8,0},{12,4},{16,24},{20,28},{24,16},{28,20},{1,9},{5... | collective-permute-start | bytes 1572872 | tf_op jit(solution)/shard_map/ppermute | solution.py:57
  114.0 13.5 %collective-permute-start.27 = (bf16[1,128,2048]{2,1,0:T(8,128)(2,1)S(1)}, bf16[1,128,2048]{2,1,0:T(8,128)(2,1)S(1)}, u32[]{:S(2)}, u32[]{:S(2)}) collective-permute-start(bf16[1,128,2048]{2,1,0:T(8,128)(2,1)S(1)} %get-tuple-element.848), channel_id=1, source_target_pairs={{0,3},{1,2},{2,1},{3,0},{4,7},{5,6},{6,5},{7,4},{8,11},{9,10},{10,... | collective-permute-start | bytes 1572872 | tf_op jit(solution)/shard_map/ppermute | solution.py:39
  114.0 14.4 %collective-permute-start.28 = (bf16[1,128,2048]{2,1,0:T(8,128)(2,1)S(1)}, bf16[1,128,2048]{2,1,0:T(8,128)(2,1)S(1)}, u32[]{:S(2)}, u32[]{:S(2)}) collective-permute-start(bf16[1,128,2048]{2,1,0:T(8,128)(2,1)S(1)} %collective-permute-done.24.refs_2_), channel_id=1, source_target_pairs={{0,4},{4,0},{8,12},{12,8},{16,20},{20,16},{24,28},{28,24},{1,5},{5... | collective-permute-start | bytes 1572872 | tf_op jit(solution)/shard_map/ppermute | solution.py:57
  115.3 14.1 %collective-permute-start.29 = (bf16[1,128,2048]{2,1,0:T(8,128)(2,1)S(1)}, bf16[1,128,2048]{2,1,0:T(8,128)(2,1)S(1)}, u32[]{:S(2)}, u32[]{:S(2)}) collective-permute-start(bf16[1,128,2048]{2,1,0:T(8,128)(2,1)S(1)} %collective-permute-done.24.refs_2_), channel_id=1, source_target_pairs={{0,8},{4,12},{8,0},{12,4},{16,24},{20,28},{24,16},{28,20},{1,9},{5... | collective-permute-start | bytes 1572872 | tf_op jit(solution)/shard_map/ppermute | solution.py:57
  132.2 15.3 %collective-permute-start.34 = (bf16[1,128,2048]{2,1,0:T(8,128)(2,1)S(1)}, bf16[1,128,2048]{2,1,0:T(8,128)(2,1)S(1)}, u32[]{:S(2)}, u32[]{:S(2)}) collective-permute-start(bf16[1,128,2048]{2,1,0:T(8,128)(2,1)S(1)} %collective-permute-done.19.refs_6_), channel_id=1, source_target_pairs={{0,4},{4,0},{8,12},{12,8},{16,20},{20,16},{24,28},{28,24},{1,5},{5... | collective-permute-start | bytes 1572872 | tf_op jit(solution)/shard_map/ppermute | solution.py:57
  133.0 14.5 %collective-permute-start.35 = (bf16[1,128,2048]{2,1,0:T(8,128)(2,1)S(1)}, bf16[1,128,2048]{2,1,0:T(8,128)(2,1)S(1)}, u32[]{:S(2)}, u32[]{:S(2)}) collective-permute-start(bf16[1,128,2048]{2,1,0:T(8,128)(2,1)S(1)} %collective-permute-done.25.refs_5_), channel_id=1, source_target_pairs={{0,8},{4,12},{8,0},{12,4},{16,24},{20,28},{24,16},{28,20},{1,9},{5... | collective-permute-start | bytes 1572872 | tf_op jit(solution)/shard_map/ppermute | solution.py:57
  225.8 17.0 %collective-permute-start.55 = (bf16[64,2048]{1,0:T(8,128)(2,1)S(1)}, bf16[64,2048]{1,0:T(8,128)(2,1)S(1)}, u32[]{:S(2)}, u32[]{:S(2)}) collective-permute-start(bf16[64,2048]{1,0:T(8,128)(2,1)S(1)} %get-tuple-element.1106.refs_0_), channel_id=1, source_target_pairs={{0,2},{1,3},{2,0},{3,1},{4,6},{5,7},{6,4},{7,5},{8,10},{9,11},{10,... | collective-permute-start | bytes 786440 | tf_op jit(solution)/shard_map/ppermute | solution.py:39
  227.1 15.8 %collective-permute-start.56 = (bf16[64,2048]{1,0:T(8,128)(2,1)S(1)}, bf16[64,2048]{1,0:T(8,128)(2,1)S(1)}, u32[]{:S(2)}, u32[]{:S(2)}) collective-permute-start(bf16[64,2048]{1,0:T(8,128)(2,1)S(1)} %get-tuple-element.1106.refs_0_), channel_id=1, source_target_pairs={{0,1},{1,0},{2,3},{3,2},{4,5},{5,4},{6,7},{7,6},{8,9},{9,8},{10,11... | collective-permute-start | bytes 786440 | tf_op jit(solution)/shard_map/ppermute | solution.py:39
  227.1 15.8 %collective-permute-start.57 = (bf16[64,2048]{1,0:T(8,128)(2,1)S(1)}, bf16[64,2048]{1,0:T(8,128)(2,1)S(1)}, u32[]{:S(2)}, u32[]{:S(2)}) collective-permute-start(bf16[64,2048]{1,0:T(8,128)(2,1)S(1)} %get-tuple-element.1080), channel_id=1, source_target_pairs={{0,0},{16,1},{4,2},{20,3},{1,4},{17,5},{5,6},{21,7},{2,8},{18,9},{... | collective-permute-start | bytes 786440 | tf_op jit(solution)/shard_map/ppermute | solution.py:1160
  250.3 16.6 %collective-permute-start.61 = (bf16[64,2048]{1,0:T(8,128)(2,1)S(1)}, bf16[64,2048]{1,0:T(8,128)(2,1)S(1)}, u32[]{:S(2)}, u32[]{:S(2)}) collective-permute-start(bf16[64,2048]{1,0:T(8,128)(2,1)S(1)} %get-tuple-element.1121), channel_id=1, source_target_pairs={{12,0},{28,1},{8,2},{24,3},{13,4},{29,5},{9,6},{25,7},{14,8},{30,9... | collective-permute-start | bytes 786440 | tf_op jit(solution)/shard_map/ppermute | solution.py:1160
  366.0 19.7 %collective-permute-start.96 = (bf16[64,2048]{1,0:T(8,128)(2,1)S(1)}, bf16[64,2048]{1,0:T(8,128)(2,1)S(1)}, u32[]{:S(2)}, u32[]{:S(2)}) collective-permute-start(bf16[64,2048]{1,0:T(8,128)(2,1)S(1)} %get-tuple-element.1387), channel_id=1, source_target_pairs={{12,0},{28,1},{8,2},{24,3},{13,4},{29,5},{9,6},{25,7},{14,8},{30,9... | collective-permute-start | bytes 786440 | tf_op jit(solution)/shard_map/ppermute | solution.py:1160
  (170 other events, 2004.8 us)

commit v2 on v1

--- a/solution.py
+++ b/solution.py
@@ -1449,16 +1449,15 @@
     broad[0] = grown(broad[0], got)
     early = (own_early + got_early.astype(F32)).astype(BF)[None]
     grad_resid[1], grad1 = back_rows(1, resid_grads[1][0], core1, got1)
-    _, [far, near, got, got_early] = side_by_side(
-        None, None, [(chip, grad1), (core, grad1), (step2, broad[0]), (step0, early)]
-    )
-    broad[0] = grown(broad[0], got)
-    early = grown(early, got_early)
+    _, [far, near, got, got_b] = side_by_side(
+        None, None, [(chip, grad1), (core, grad1), (step2, broad[0]), (step1, broad[1])]
+    )
+    broad = [grown(broad[0], got), grown(broad[1], got_b)]
     _, [cross] = side_by_side(None, None, [(core, far)])
     out_grads[1] = back_out(1, [grad1, far, near, cross])
     grad_mixed = jnp.concatenate([g[0] for g in out_grads])
 
-    attention_sends = [(step1, broad[1])]
+    attention_sends = [(step0, early)]
     if simple:
         (query_turned, key_turned, grad_values, inner), [got] = side_by_side(
             lambda x: attention_back(
@@ -1470,7 +1469,7 @@
     else:
         query_turned, key_turned, grad_values, inner = attention_grads(grad_mixed)
         [got] = [send(value) for send, value in attention_sends]
-    broad[1] = grown(broad[1], got)
+    early = grown(early, got)
     inners, _ = from_all(inner, [])
     grads, lows, down_late, up_late = qkv_grads(
         [query_turned, key_turned], grad_values, pre, squares, inners, token_parts, qkv_low, own_model, chunks

time: 392 us -> 394 us (level)
  waiting for transfers between devices: 153 us -> 160 us
  starting transfers between devices: 112 us -> 108 us
    ppermute x32, waiting for transfers between devices: 59.4 us -> 66 us  [over_ctx(): return lax.ppermute(value, 'ctx', [(i, i ^ flip) for i in range(size)])]
  transfers between devices with their start and end apart: 97 -> 97, of which waited for: 53 -> 49; matrix products, arithmetic and copies ran while one was open for 1% -> 1% of each run, Pallas kernels for 24% -> 24%
where the time goes in v2:
time: 394 us; the launch traced here: 389 us
  waiting for transfers between devices  160 us (41%)
  starting transfers between devices  108 us (27%)
  Pallas kernels  106 us (27%)
  local copies, waits for them, and re-layouts  7.24 us (2%)
  other arithmetic  4.92 us (1%)
    pallas_call x41, Pallas kernels, call(): pl.pallas_call(body, grid_spec=pltpu.PrefetchScalarGridSpec(num_scalar_pr...  106 us
    ppermute x32, waiting for transfers between devices, over_ctx(): return lax.ppermute(value, 'ctx', [(i, i ^ flip) for i in range(size)])  66 us
    ppermute x57, waiting for transfers between devices, over_shard(): return lax.ppermute(value, 'shard', [(i, i ^ flip) for i in range(size)])  64.4 us
    ppermute x57, starting transfers between devices, over_shard(): return lax.ppermute(value, 'shard', [(i, i ^ flip) for i in range(size)])  48.1 us
    ppermute x32, starting transfers between devices, over_ctx(): return lax.ppermute(value, 'ctx', [(i, i ^ flip) for i in range(size)])  30.8 us
    ppermute x4, waiting for transfers between devices, return_row(): lax.ppermute(cut, ('ctx', 'shard'), [(b, a) for a, b in pairs[p]])  21.8 us
    ppermute x4, starting transfers between devices, return_row(): lax.ppermute(cut, ('ctx', 'shard'), [(b, a) for a, b in pairs[p]])  17.1 us
    ppermute x4, starting transfers between devices, send_row(): return lambda cut: lax.ppermute(cut, ('ctx', 'shard'), pairs[p])  12 us
  transfers between devices with their start and end apart: 97, of which 49 were waited for; matrix products, arithmetic and copies ran while one was open for 1% of the time, Pallas kernels for 24%

profile of v2, /device:TPU:0, one launch (start us, length us, event | category | flops | bytes accessed | tf_op | source)
XLA Modules:
  0.0 389.1 jit_solution(9542285735962586388)
XLA Ops:
  12.4 5.7 %collective-permute-start.5 = (bf16[64,2048]{1,0:T(8,128)(2,1)S(1)}, bf16[64,2048]{1,0:T(8,128)(2,1)S(1)}, u32[]{:S(2)}, u32[]{:S(2)}) collective-permute-start(bf16[64,2048]{1,0:T(8,128)(2,1)S(1)} %get-tuple-element.748), channel_id=1, source_target_pairs={{0,12},{1,28},{2,8},{3,24},{4,13},{5,29},{6,9},{7,25},{8,14},{9,30... | collective-permute-start | bytes 786440 | tf_op jit(solution)/shard_map/ppermute | solution.py:1151
  25.2 6.4 %collective-permute-done.5 = bf16[64,2048]{1,0:T(8,128)(2,1)S(1)} collective-permute-done((bf16[64,2048]{1,0:T(8,128)(2,1)S(1)}, bf16[64,2048]{1,0:T(8,128)(2,1)S(1)}, u32[]{:S(2)}, u32[]{:S(2)}) %collective-permute-start.5) | collective-permute-done | bytes 262176 | tf_op jit(solution)/shard_map/ppermute | solution.py:1151
  49.5 7.6 %collective-permute-done.11.refs_8_ = bf16[3,128,512]{2,1,0:T(8,128)(2,1)S(1)} collective-permute-done((bf16[3,128,512]{2,1,0:T(8,128)(2,1)S(1)}, bf16[3,128,512]{2,1,0:T(8,128)(2,1)S(1)}, u32[]{:S(2)}, u32[]{:S(2)}) %collective-permute-start.11) | collective-permute-done | bytes 393248 | tf_op jit(solution)/shard_map/ppermute | solution.py:57
  66.2 8.3 %collective-permute-done.13.refs_11_ = bf16[3,128,512]{2,1,0:T(8,128)(2,1)S(1)} collective-permute-done((bf16[3,128,512]{2,1,0:T(8,128)(2,1)S(1)}, bf16[3,128,512]{2,1,0:T(8,128)(2,1)S(1)}, u32[]{:S(2)}, u32[]{:S(2)}) %collective-permute-start.13) | collective-permute-done | bytes 393248 | tf_op jit(solution)/shard_map/ppermute | solution.py:57
  81.3 11.9 %shard_map.212 = (bf16[3,512,512]{2,1,0:T(8,128)(2,1)S(1)}, bf16[3,512,16]{2,1,0:T(8,128)(2,1)S(1)}, f32[24,512]{1,0:T(8,128)S(1)}, bf16[3,2048,512]{2,1,0:T(8,128)(2,1)}) custom-call(s32[2]{0:T(128)S(1)} %pad_add_fusion.places, bf16[160,2048]{1,0:T(8,128)(2,1)S(1)} %pad_maximum_fusion.3.refs_0_.refs_13_, ...), custom_call_target="tpu_custom_call" | custom-call | flops 3221225472 | tf_op jit(solution)/shard_map/pallas_call | solution.py:71
  100.9 6.2 %shard_map.213 = (bf16[512,512]{1,0:T(8,128)(2,1)S(1)}, bf16[512,512]{1,0:T(8,128)(2,1)S(1)}, bf16[512,512]{1,0:T(8,128)(2,1)S(1)}, f32[32,512]{1,0:T(8,128)S(1)}) custom-call(bf16[3,512,512]{2,1,0:T(8,128)(2,1)S(1)} %get-tuple-element.820.refs_0_.refs_1_.refs_2_.refs_3_.refs_4_, ...), custom_call_target="tpu_custom_call" | custom-call | flops 536870912 | tf_op jit(solution)/shard_map/pallas_call | solution.py:71
  119.4 8.1 %collective-permute-done.27.refs_3_ = bf16[1,128,2048]{2,1,0:T(8,128)(2,1)S(1)} collective-permute-done((bf16[1,128,2048]{2,1,0:T(8,128)(2,1)S(1)}, bf16[1,128,2048]{2,1,0:T(8,128)(2,1)S(1)}, u32[]{:S(2)}, u32[]{:S(2)}) %collective-permute-start.27) | collective-permute-done | bytes 524320 | tf_op jit(solution)/shard_map/ppermute | solution.py:39
  151.6 4.8 %collective-permute-done.36.refs_1_ = bf16[64,2048]{1,0:T(8,128)(2,1)S(1)} collective-permute-done((bf16[64,2048]{1,0:T(8,128)(2,1)S(1)}, bf16[64,2048]{1,0:T(8,128)(2,1)S(1)}, u32[]{:S(2)}, u32[]{:S(2)}) %collective-permute-start.36) | collective-permute-done | bytes 262176 | tf_op jit(solution)/shard_map/ppermute | solution.py:39
  165.6 6.1 %collective-permute-done.41.refs_1_ = bf16[64,2048]{1,0:T(8,128)(2,1)S(1)} collective-permute-done((bf16[64,2048]{1,0:T(8,128)(2,1)S(1)}, bf16[64,2048]{1,0:T(8,128)(2,1)S(1)}, u32[]{:S(2)}, u32[]{:S(2)}) %collective-permute-start.41) | collective-permute-done | bytes 262176 | tf_op jit(solution)/shard_map/ppermute | solution.py:39
  175.6 5.9 %shard_map.223 = (bf16[256,2048]{1,0:T(8,128)(2,1)S(1)}, bf16[256,2048]{1,0:T(8,128)(2,1)S(1)}, bf16[256,2048]{1,0:T(8,128)(2,1)S(1)}, bf16[256,32]{1,0:T(8,128)(2,1)S(1)}) custom-call(bf16[64,2048]{1,0:T(8,128)(2,1)S(1)} %get-tuple-element.941.refs_0_, bf16[64,2048]{1,0:T(8,128)(2,1)S(1)} %collective-permute-done.36.refs_1_, ...), custom_call_target="tpu_custom_call" | custom-call | flops 4294967296 | tf_op jit(solution)/shard_map/pallas_call | solution.py:71
  197.5 5.9 %shard_map.226 = (bf16[256,2048]{1,0:T(8,128)(2,1)S(1)}, bf16[256,2048]{1,0:T(8,128)(2,1)S(1)}, bf16[256,2048]{1,0:T(8,128)(2,1)S(1)}, bf16[256,32]{1,0:T(8,128)(2,1)S(1)}) custom-call(bf16[64,2048]{1,0:T(8,128)(2,1)S(1)} %get-tuple-element.987.refs_0_, bf16[64,2048]{1,0:T(8,128)(2,1)S(1)} %collective-permute-done.41.refs_1_, ...), custom_call_target="tpu_custom_call" | custom-call | flops 4294967296 | tf_op jit(solution)/shard_map/pallas_call | solution.py:71
  218.1 5.1 %shard_map.230 = (bf16[256,2048]{1,0:T(8,128)(2,1)S(1)}, bf16[256,2048]{1,0:T(8,128)(2,1)S(1)}, bf16[256,32]{1,0:T(8,128)(2,1)S(1)}, f32[16,2048]{1,0:T(8,128)S(...) custom-call(bf16[64,2048]{1,0:T(8,128)(2,1)S(1)} %get-tuple-element.1041.refs_0_, ...), custom_call_target="tpu_custom_call" | custom-call | flops 2147483648 | tf_op jit(solution)/shard_map/pallas_call | solution.py:71
  227.1 10.4 %collective-permute-start.57 = (bf16[64,2048]{1,0:T(8,128)(2,1)S(1)}, bf16[64,2048]{1,0:T(8,128)(2,1)S(1)}, u32[]{:S(2)}, u32[]{:S(2)}) collective-permute-start(bf16[64,2048]{1,0:T(8,128)(2,1)S(1)} %get-tuple-element.1080), channel_id=1, source_target_pairs={{0,0},{16,1},{4,2},{20,3},{1,4},{17,5},{5,6},{21,7},{2,8},{18,9},{... | collective-permute-start | bytes 786440 | tf_op jit(solution)/shard_map/ppermute | solution.py:1160
  237.5 5.3 %shard_map.232 = (bf16[128,2048]{1,0:T(8,128)(2,1)S(1)}, bf16[128,2048]{1,0:T(8,128)(2,1)S(1)}, f32[32,2048]{1,0:T(8,128)S(1)}) custom-call(bf16[256,2048]{1,0:T(8,128)(2,1)S(1)} %get-tuple-element.1072.gate_grad, bf16[256,2048]{1,0:T(8,128)(2,1)S(1)} %get-tuple-element.1073.upper_grad, ...), custom_call_target="tpu_custom_call" | custom-call | flops 4294967296 | tf_op jit(solution)/shard_map/pallas_call | solution.py:71
  253.7 5.2 %shard_map.234 = (bf16[256,2048]{1,0:T(8,128)(2,1)S(1)}, bf16[256,2048]{1,0:T(8,128)(2,1)S(1)}, bf16[256,32]{1,0:T(8,128)(2,1)S(1)}, f32[16,2048]{1,0:T(8,128)S(...) custom-call(bf16[64,2048]{1,0:T(8,128)(2,1)S(1)} %get-tuple-element.1106.refs_0_, ...), custom_call_target="tpu_custom_call" | custom-call | flops 2147483648 | tf_op jit(solution)/shard_map/pallas_call | solution.py:71
  258.9 7.9 %collective-permute-done.61 = bf16[64,2048]{1,0:T(8,128)(2,1)S(1)} collective-permute-done((bf16[64,2048]{1,0:T(8,128)(2,1)S(1)}, bf16[64,2048]{1,0:T(8,128)(2,1)S(1)}, u32[]{:S(2)}, u32[]{:S(2)}) %collective-permute-start.61) | collective-permute-done | bytes 262176 | tf_op jit(solution)/shard_map/ppermute | solution.py:1160
  270.5 5.3 %shard_map.236 = (bf16[128,2048]{1,0:T(8,128)(2,1)S(1)}, bf16[128,2048]{1,0:T(8,128)(2,1)S(1)}, f32[32,2048]{1,0:T(8,128)S(1)}) custom-call(bf16[256,2048]{1,0:T(8,128)(2,1)S(1)} %get-tuple-element.1147.gate_grad, bf16[256,2048]{1,0:T(8,128)(2,1)S(1)} %get-tuple-element.1148.upper_grad, ...), custom_call_target="tpu_custom_call" | custom-call | flops 4294967296 | tf_op jit(solution)/shard_map/pallas_call | solution.py:71
  282.5 5.7 %collective-permute-done.70 = bf16[48,512]{1,0:T(8,128)(2,1)S(1)} collective-permute-done((bf16[48,512]{1,0:T(8,128)(2,1)S(1)}, bf16[48,512]{1,0:T(8,128)(2,1)S(1)}, u32[]{:S(2)}, u32[]{:S(2)}) %collective-permute-start.70) | collective-permute-done | bytes 49184 | tf_op jit(solution)/shard_map/ppermute | solution.py:39
  294.1 10.4 %collective-permute-done.75 = bf16[2,48,1024]{2,1,0:T(8,128)(2,1)S(1)} collective-permute-done((bf16[2,48,1024]{2,1,0:T(8,128)(2,1)S(1)}, bf16[2,48,1024]{2,1,0:T(8,128)(2,1)S(1)}, u32[]{:S(2)}, u32[]{:S(2)}) %collective-permute-start.75) | collective-permute-done | bytes 196640 | tf_op jit(solution)/shard_map/ppermute | solution.py:57
  308.0 7.5 %shard_map.241 = (bf16[512,512]{1,0:T(8,128)(2,1)S(1)}, bf16[512,512]{1,0:T(8,128)(2,1)S(1)}, bf16[512,512]{1,0:T(8,128)(2,1)S(1)}, f32[16,512]{1,0:T(8,128)S(1)}) custom-call(bf16[512,512]{1,0:T(8,128)(2,1)S(1)} %copy-done.32, bf16[512,512]{1,0:T(8,128)(2,1)S(1)} %copy-done.34, ...), custom_call_target="tpu_custom_call" | custom-call | flops 1342177280 | tf_op jit(solution)/shard_map/pallas_call | solution.py:71
  334.8 5.5 %collective-permute-done.86 = bf16[1,128,512]{2,1,0:T(8,128)(2,1)S(1)} collective-permute-done((bf16[1,128,512]{2,1,0:T(8,128)(2,1)S(1)}, bf16[1,128,512]{2,1,0:T(8,128)(2,1)S(1)}, u32[]{:S(2)}, u32[]{:S(2)}) %collective-permute-start.86) | collective-permute-done | bytes 131104 | tf_op jit(solution)/shard_map/ppermute | solution.py:57
  343.5 7.5 %collective-permute-done.89 = bf16[2,128,256]{2,1,0:T(8,128)(2,1)S(1)} collective-permute-done((bf16[2,128,256]{2,1,0:T(8,128)(2,1)S(1)}, bf16[2,128,256]{2,1,0:T(8,128)(2,1)S(1)}, u32[]{:S(2)}, u32[]{:S(2)}) %collective-permute-start.89) | collective-permute-done | bytes 131104 | tf_op jit(solution)/shard_map/ppermute | solution.py:57
  362.4 5.0 %collective-permute-done.94 = bf16[4,128,256]{2,1,0:T(8,128)(2,1)S(1)} collective-permute-done((bf16[4,128,256]{2,1,0:T(8,128)(2,1)S(1)}, bf16[4,128,256]{2,1,0:T(8,128)(2,1)S(1)}, u32[]{:S(2)}, u32[]{:S(2)}) %collective-permute-start.94) | collective-permute-done | bytes 262176 | tf_op jit(solution)/shard_map/ppermute | solution.py:57
  374.0 13.8 %collective-permute-done.96.refs_1_ = bf16[64,2048]{1,0:T(8,128)(2,1)S(1)} collective-permute-done((bf16[64,2048]{1,0:T(8,128)(2,1)S(1)}, bf16[64,2048]{1,0:T(8,128)(2,1)S(1)}, u32[]{:S(2)}, u32[]{:S(2)}) %collective-permute-start.96) | collective-permute-done | bytes 262176 | tf_op jit(solution)/shard_map/ppermute | solution.py:1160
  (472 shorter events, 214.5 us)
Async XLA Ops:
  9.7 22.3 %collective-permute-start.6 = (bf16[3,512,512]{2,1,0:T(8,128)(2,1)S(1)}, bf16[3,512,512]{2,1,0:T(8,128)(2,1)S(1)}, u32[]{:S(2)}, u32[]{:S(2)}) collective-permute-start(bf16[3,512,512]{2,1,0:T(8,128)(2,1)S(1)} %get-tuple-element.749), channel_id=1, source_target_pairs={{0,1},{1,0},{2,3},{3,2},{4,5},{5,4},{6,7},{7,6},{8,9},{9,8},{10,11... | collective-permute-start | bytes 4718600 | tf_op jit(solution)/shard_map/ppermute | solution.py:39
  10.0 21.9 %collective-permute-start.3 = (bf16[3,128,512]{2,1,0:T(8,128)(2,1)S(1)}, bf16[3,128,512]{2,1,0:T(8,128)(2,1)S(1)}, u32[]{:S(2)}, u32[]{:S(2)}) collective-permute-start(bf16[3,128,512]{2,1,0:T(8,128)(2,1)S(1)} %get-tuple-element.746), channel_id=1, source_target_pairs={{0,2},{1,3},{2,0},{3,1},{4,6},{5,7},{6,4},{7,5},{8,10},{9,11},{10,... | collective-permute-start | bytes 1179656 | tf_op jit(solution)/shard_map/ppermute | solution.py:39
  11.7 13.5 %collective-permute-start.4 = (bf16[64,2048]{1,0:T(8,128)(2,1)S(1)}, bf16[64,2048]{1,0:T(8,128)(2,1)S(1)}, u32[]{:S(2)}, u32[]{:S(2)}) collective-permute-start(bf16[64,2048]{1,0:T(8,128)(2,1)S(1)} %get-tuple-element.747), channel_id=1, source_target_pairs={{0,0},{1,16},{2,4},{3,20},{4,1},{5,17},{6,5},{7,21},{8,2},{9,18},{... | collective-permute-start | bytes 786440 | tf_op jit(solution)/shard_map/ppermute | solution.py:1151
  12.4 19.2 %collective-permute-start.5 = (bf16[64,2048]{1,0:T(8,128)(2,1)S(1)}, bf16[64,2048]{1,0:T(8,128)(2,1)S(1)}, u32[]{:S(2)}, u32[]{:S(2)}) collective-permute-start(bf16[64,2048]{1,0:T(8,128)(2,1)S(1)} %get-tuple-element.748), channel_id=1, source_target_pairs={{0,12},{1,28},{2,8},{3,24},{4,13},{5,29},{6,9},{7,25},{8,14},{9,30... | collective-permute-start | bytes 786440 | tf_op jit(solution)/shard_map/ppermute | solution.py:1151
  45.9 16.5 %collective-permute-start.10 = (bf16[160,2048]{1,0:T(8,128)(2,1)S(1)}, bf16[160,2048]{1,0:T(8,128)(2,1)S(1)}, u32[]{:S(2)}, u32[]{:S(2)}) collective-permute-start(bf16[160,2048]{1,0:T(8,128)(2,1)S(1)} %pad_maximum_fusion.3.refs_0_.refs_13_), channel_id=1, source_target_pairs={{0,2},{1,3},{2,0},{3,1},{4,6},{5,7},{6,4},{7,5},{8,10},{9,11},{10,... | collective-permute-start | bytes 1966088 | tf_op jit(solution)/shard_map/ppermute | solution.py:39
  62.5 14.4 %collective-permute-start.15 = (bf16[2,160,2048]{2,1,0:T(8,128)(2,1)S(1)}, bf16[2,160,2048]{2,1,0:T(8,128)(2,1)S(1)}, u32[]{:S(2)}, u32[]{:S(2)}) collective-permute-start(bf16[2,160,2048]{2,1,0:T(8,128)(2,1)S(1)} %pad_maximum_fusion), channel_id=1, source_target_pairs={{0,1},{1,0},{2,3},{3,2},{4,5},{5,4},{6,7},{7,6},{8,9},{9,8},{10,11... | collective-permute-start | bytes 3932168 | tf_op jit(solution)/shard_map/ppermute | solution.py:39
  62.6 14.3 %collective-permute-start.16 = (bf16[1,128,2048]{2,1,0:T(8,128)(2,1)S(1)}, bf16[1,128,2048]{2,1,0:T(8,128)(2,1)S(1)}, u32[]{:S(2)}, u32[]{:S(2)}) collective-permute-start(bf16[1,128,2048]{2,1,0:T(8,128)(2,1)S(1)} %get-tuple-element.780), channel_id=1, source_target_pairs={{0,2},{1,3},{2,0},{3,1},{4,6},{5,7},{6,4},{7,5},{8,10},{9,11},{10,... | collective-permute-start | bytes 1572872 | tf_op jit(solution)/shard_map/ppermute | solution.py:39
  76.9 17.1 %collective-permute-start.20 = (bf16[2,512,2048]{2,1,0:T(8,128)(2,1)S(1)}, bf16[2,512,2048]{2,1,0:T(8,128)(2,1)S(1)}, u32[]{:S(2)}, u32[]{:S(2)}) collective-permute-start(bf16[2,512,2048]{2,1,0:T(8,128)(2,1)S(1)} %get-tuple-element.803), channel_id=1, source_target_pairs={{0,1},{1,0},{2,3},{3,2},{4,5},{5,4},{6,7},{7,6},{8,9},{9,8},{10,11... | collective-permute-start | bytes 12582920 | tf_op jit(solution)/shard_map/ppermute | solution.py:39
  77.0 17.0 %collective-permute-start.17 = (bf16[1,128,2048]{2,1,0:T(8,128)(2,1)S(1)}, bf16[1,128,2048]{2,1,0:T(8,128)(2,1)S(1)}, u32[]{:S(2)}, u32[]{:S(2)}) collective-permute-start(bf16[1,128,2048]{2,1,0:T(8,128)(2,1)S(1)} %get-tuple-element.800), channel_id=1, source_target_pairs={{0,3},{1,2},{2,1},{3,0},{4,7},{5,6},{6,5},{7,4},{8,11},{9,10},{10,... | collective-permute-start | bytes 1572872 | tf_op jit(solution)/shard_map/ppermute | solution.py:39
  77.9 16.1 %collective-permute-start.18 = (bf16[1,128,2048]{2,1,0:T(8,128)(2,1)S(1)}, bf16[1,128,2048]{2,1,0:T(8,128)(2,1)S(1)}, u32[]{:S(2)}, u32[]{:S(2)}) collective-permute-start(bf16[1,128,2048]{2,1,0:T(8,128)(2,1)S(1)} %collective-permute-done.16.refs_2_), channel_id=1, source_target_pairs={{0,4},{4,0},{8,12},{12,8},{16,20},{20,16},{24,28},{28,24},{1,5},{5... | collective-permute-start | bytes 1572872 | tf_op jit(solution)/shard_map/ppermute | solution.py:57
  79.0 15.0 %collective-permute-start.19 = (bf16[1,128,2048]{2,1,0:T(8,128)(2,1)S(1)}, bf16[1,128,2048]{2,1,0:T(8,128)(2,1)S(1)}, u32[]{:S(2)}, u32[]{:S(2)}) collective-permute-start(bf16[1,128,2048]{2,1,0:T(8,128)(2,1)S(1)} %collective-permute-done.16.refs_2_), channel_id=1, source_target_pairs={{0,8},{4,12},{8,0},{12,4},{16,24},{20,28},{24,16},{28,20},{1,9},{5... | collective-permute-start | bytes 1572872 | tf_op jit(solution)/shard_map/ppermute | solution.py:57
  98.2 14.0 %collective-permute-start.24 = (bf16[1,128,2048]{2,1,0:T(8,128)(2,1)S(1)}, bf16[1,128,2048]{2,1,0:T(8,128)(2,1)S(1)}, u32[]{:S(2)}, u32[]{:S(2)}) collective-permute-start(bf16[1,128,2048]{2,1,0:T(8,128)(2,1)S(1)} %get-tuple-element.831), channel_id=1, source_target_pairs={{0,2},{1,3},{2,0},{3,1},{4,6},{5,7},{6,4},{7,5},{8,10},{9,11},{10,... | collective-permute-start | bytes 1572872 | tf_op jit(solution)/shard_map/ppermute | solution.py:39
  99.5 14.1 %collective-permute-start.25 = (bf16[1,128,2048]{2,1,0:T(8,128)(2,1)S(1)}, bf16[1,128,2048]{2,1,0:T(8,128)(2,1)S(1)}, u32[]{:S(2)}, u32[]{:S(2)}) collective-permute-start(bf16[1,128,2048]{2,1,0:T(8,128)(2,1)S(1)} %collective-permute-done.17.refs_3_), channel_id=1, source_target_pairs={{0,4},{4,0},{8,12},{12,8},{16,20},{20,16},{24,28},{28,24},{1,5},{5... | collective-permute-start | bytes 1572872 | tf_op jit(solution)/shard_map/ppermute | solution.py:57
  100.3 13.8 %collective-permute-start.26 = (bf16[1,128,2048]{2,1,0:T(8,128)(2,1)S(1)}, bf16[1,128,2048]{2,1,0:T(8,128)(2,1)S(1)}, u32[]{:S(2)}, u32[]{:S(2)}) collective-permute-start(bf16[1,128,2048]{2,1,0:T(8,128)(2,1)S(1)} %collective-permute-done.17.refs_3_), channel_id=1, source_target_pairs={{0,8},{4,12},{8,0},{12,4},{16,24},{20,28},{24,16},{28,20},{1,9},{5... | collective-permute-start | bytes 1572872 | tf_op jit(solution)/shard_map/ppermute | solution.py:57
  114.0 13.5 %collective-permute-start.27 = (bf16[1,128,2048]{2,1,0:T(8,128)(2,1)S(1)}, bf16[1,128,2048]{2,1,0:T(8,128)(2,1)S(1)}, u32[]{:S(2)}, u32[]{:S(2)}) collective-permute-start(bf16[1,128,2048]{2,1,0:T(8,128)(2,1)S(1)} %get-tuple-element.848), channel_id=1, source_target_pairs={{0,3},{1,2},{2,1},{3,0},{4,7},{5,6},{6,5},{7,4},{8,11},{9,10},{10,... | collective-permute-start | bytes 1572872 | tf_op jit(solution)/shard_map/ppermute | solution.py:39
  114.0 14.4 %collective-permute-start.28 = (bf16[1,128,2048]{2,1,0:T(8,128)(2,1)S(1)}, bf16[1,128,2048]{2,1,0:T(8,128)(2,1)S(1)}, u32[]{:S(2)}, u32[]{:S(2)}) collective-permute-start(bf16[1,128,2048]{2,1,0:T(8,128)(2,1)S(1)} %collective-permute-done.24.refs_2_), channel_id=1, source_target_pairs={{0,4},{4,0},{8,12},{12,8},{16,20},{20,16},{24,28},{28,24},{1,5},{5... | collective-permute-start | bytes 1572872 | tf_op jit(solution)/shard_map/ppermute | solution.py:57
  115.3 14.1 %collective-permute-start.29 = (bf16[1,128,2048]{2,1,0:T(8,128)(2,1)S(1)}, bf16[1,128,2048]{2,1,0:T(8,128)(2,1)S(1)}, u32[]{:S(2)}, u32[]{:S(2)}) collective-permute-start(bf16[1,128,2048]{2,1,0:T(8,128)(2,1)S(1)} %collective-permute-done.24.refs_2_), channel_id=1, source_target_pairs={{0,8},{4,12},{8,0},{12,4},{16,24},{20,28},{24,16},{28,20},{1,9},{5... | collective-permute-start | bytes 1572872 | tf_op jit(solution)/shard_map/ppermute | solution.py:57
  132.2 15.3 %collective-permute-start.34 = (bf16[1,128,2048]{2,1,0:T(8,128)(2,1)S(1)}, bf16[1,128,2048]{2,1,0:T(8,128)(2,1)S(1)}, u32[]{:S(2)}, u32[]{:S(2)}) collective-permute-start(bf16[1,128,2048]{2,1,0:T(8,128)(2,1)S(1)} %collective-permute-done.19.refs_6_), channel_id=1, source_target_pairs={{0,4},{4,0},{8,12},{12,8},{16,20},{20,16},{24,28},{28,24},{1,5},{5... | collective-permute-start | bytes 1572872 | tf_op jit(solution)/shard_map/ppermute | solution.py:57
  133.0 14.5 %collective-permute-start.35 = (bf16[1,128,2048]{2,1,0:T(8,128)(2,1)S(1)}, bf16[1,128,2048]{2,1,0:T(8,128)(2,1)S(1)}, u32[]{:S(2)}, u32[]{:S(2)}) collective-permute-start(bf16[1,128,2048]{2,1,0:T(8,128)(2,1)S(1)} %collective-permute-done.25.refs_5_), channel_id=1, source_target_pairs={{0,8},{4,12},{8,0},{12,4},{16,24},{20,28},{24,16},{28,20},{1,9},{5... | collective-permute-start | bytes 1572872 | tf_op jit(solution)/shard_map/ppermute | solution.py:57
  225.8 17.0 %collective-permute-start.55 = (bf16[64,2048]{1,0:T(8,128)(2,1)S(1)}, bf16[64,2048]{1,0:T(8,128)(2,1)S(1)}, u32[]{:S(2)}, u32[]{:S(2)}) collective-permute-start(bf16[64,2048]{1,0:T(8,128)(2,1)S(1)} %get-tuple-element.1106.refs_0_), channel_id=1, source_target_pairs={{0,2},{1,3},{2,0},{3,1},{4,6},{5,7},{6,4},{7,5},{8,10},{9,11},{10,... | collective-permute-start | bytes 786440 | tf_op jit(solution)/shard_map/ppermute | solution.py:39
  227.1 15.8 %collective-permute-start.56 = (bf16[64,2048]{1,0:T(8,128)(2,1)S(1)}, bf16[64,2048]{1,0:T(8,128)(2,1)S(1)}, u32[]{:S(2)}, u32[]{:S(2)}) collective-permute-start(bf16[64,2048]{1,0:T(8,128)(2,1)S(1)} %get-tuple-element.1106.refs_0_), channel_id=1, source_target_pairs={{0,1},{1,0},{2,3},{3,2},{4,5},{5,4},{6,7},{7,6},{8,9},{9,8},{10,11... | collective-permute-start | bytes 786440 | tf_op jit(solution)/shard_map/ppermute | solution.py:39
  227.1 15.8 %collective-permute-start.57 = (bf16[64,2048]{1,0:T(8,128)(2,1)S(1)}, bf16[64,2048]{1,0:T(8,128)(2,1)S(1)}, u32[]{:S(2)}, u32[]{:S(2)}) collective-permute-start(bf16[64,2048]{1,0:T(8,128)(2,1)S(1)} %get-tuple-element.1080), channel_id=1, source_target_pairs={{0,0},{16,1},{4,2},{20,3},{1,4},{17,5},{5,6},{21,7},{2,8},{18,9},{... | collective-permute-start | bytes 786440 | tf_op jit(solution)/shard_map/ppermute | solution.py:1160
  250.3 16.5 %collective-permute-start.61 = (bf16[64,2048]{1,0:T(8,128)(2,1)S(1)}, bf16[64,2048]{1,0:T(8,128)(2,1)S(1)}, u32[]{:S(2)}, u32[]{:S(2)}) collective-permute-start(bf16[64,2048]{1,0:T(8,128)(2,1)S(1)} %get-tuple-element.1121), channel_id=1, source_target_pairs={{12,0},{28,1},{8,2},{24,3},{13,4},{29,5},{9,6},{25,7},{14,8},{30,9... | collective-permute-start | bytes 786440 | tf_op jit(solution)/shard_map/ppermute | solution.py:1160
  368.2 19.7 %collective-permute-start.96 = (bf16[64,2048]{1,0:T(8,128)(2,1)S(1)}, bf16[64,2048]{1,0:T(8,128)(2,1)S(1)}, u32[]{:S(2)}, u32[]{:S(2)}) collective-permute-start(bf16[64,2048]{1,0:T(8,128)(2,1)S(1)} %get-tuple-element.1387), channel_id=1, source_target_pairs={{12,0},{28,1},{8,2},{24,3},{13,4},{29,5},{9,6},{25,7},{14,8},{30,9... | collective-permute-start | bytes 786440 | tf_op jit(solution)/shard_map/ppermute | solution.py:1160
  (170 other events, 2012.0 us)
